TPU v7x, 256 devices: a whole 4x4x8 slice. The times are simulated.
256 devices in a mesh: band: 8 (over z), tile: 32 (over x, y, core).
Axes of the slice: x: 4, y: 4, z: 8, core: 2. Of those that a mesh axis runs over, the one named last changes fastest.
Arguments:
- queries: bfloat16 [2048, 512], replicated, may hold values from -15 to 15
- query_pos: bfloat16 [2048, 512], replicated, may hold values from -6 to 6
- patches: bfloat16 [131072, 512], P(('band', 'tile')), may hold values from -6 to 6
- patch_level: int32 [131072], P(('band', 'tile')), may hold values from 0 to 3
- patch_sheet: int32 [131072], P(('band', 'tile')), may hold values from 0 to 15, as said below
- query_sheets: int32 [2048, 16], replicated, may hold values from 0 to 1, as said below
- level_embed: bfloat16 [4, 512], replicated, may hold values from -6 to 6
- cross_proj: bfloat16 [4, 512, 512], replicated, may hold values from -0.25 to 0.25
- self_proj: bfloat16 [4, 512, 512], replicated, may hold values from -0.25 to 0.25
- mlp_in: bfloat16 [512, 2048], replicated, may hold values from -0.25 to 0.25
- mlp_out: bfloat16 [2048, 512], replicated, may hold values from -0.125 to 0.125
- norm_gain: float32 [3, 512], replicated, may hold values from 0.5 to 1.5
Outputs:
- decoded: bfloat16 [2048, 512], P('tile')
Inputs may be any that keep to these rules, and one draw needn't show every extreme that they name: `patch_sheet`: the patches of rows b * 16384 to (b + 1) * 16384 - 1 lie on sheets b * 2 to (b + 1) * 2 - 1, and each of these sheets holds one or more of them. `query_sheets`: every query may look at one sheet or more.
All inputs are finite; a program needn't handle non-finite values.
Results may differ from a plain program's by a relative error of at most 0.025.
Values may be sent and summed in bfloat16 or wider, within the bound.
No kernel may reach another device: no remote copies, remote signals or barrier semaphores. Data moves between devices by JAX's collectives and lax.ppermute only.
A program may use at most 192 MiB of HBM per device.

v0:
```python
import math

import jax
import jax.numpy as jnp
from jax import lax
from jax.sharding import PartitionSpec as P

HEADS = 8


def layer_norm(values, gain):
    center = jnp.mean(values, axis=-1, keepdims=True)
    shifted = values - center
    spread = jnp.mean(shifted * shifted, axis=-1, keepdims=True)
    return shifted * lax.rsqrt(spread + 1e-05) * gain


def self_attend(q_self, k_self, v_self, head_size):
    rows = q_self.shape[0]
    keys = k_self.shape[0]
    q_heads = q_self.reshape(rows, -1, head_size)
    k_heads = k_self.reshape(keys, -1, head_size)
    v_heads = v_self.reshape(keys, -1, head_size)
    scores = jnp.einsum("qhe,khe->hqk", q_heads, k_heads, preferred_element_type=jnp.float32)
    peak = jnp.max(scores, axis=-1, keepdims=True)
    weights = jnp.exp(scores - peak)
    probs = (weights / jnp.sum(weights, axis=-1, keepdims=True)).astype(jnp.bfloat16)
    result = jnp.einsum("hqk,khe->qhe", probs, v_heads, preferred_element_type=jnp.float32)
    return result.reshape(rows, -1).astype(jnp.bfloat16)


def body(
    queries,
    query_pos,
    patches,
    patch_level,
    patch_sheet,
    query_sheets,
    level_embed,
    cross_proj,
    self_proj,
    mlp_in,
    mlp_out,
    norm_gain,
):
    tiles = lax.axis_size("tile")
    total_q, width = queries.shape
    head_size = width // HEADS
    local_rows = patches.shape[0]
    score_scale = 1.0 / math.sqrt(head_size)
    mixed_in = queries + query_pos
    q_cross = (
        jnp.dot(mixed_in, cross_proj[0], preferred_element_type=jnp.float32) * score_scale
    ).astype(jnp.bfloat16)
    level_rows = (
        patch_level[:, None] == jnp.arange(level_embed.shape[0], dtype=jnp.int32)[None, :]
    ).astype(jnp.bfloat16)
    key_input = (
        patches.astype(jnp.float32)
        + jnp.dot(level_rows, level_embed, preferred_element_type=jnp.float32)
    ).astype(jnp.bfloat16)
    k_cross = jnp.dot(key_input, cross_proj[1], preferred_element_type=jnp.float32).astype(
        jnp.bfloat16
    )
    v_cross = jnp.dot(patches, cross_proj[2], preferred_element_type=jnp.float32).astype(
        jnp.bfloat16
    )
    sheet_rows = (
        patch_sheet[:, None] == jnp.arange(query_sheets.shape[1], dtype=jnp.int32)[None, :]
    ).astype(jnp.bfloat16)
    q_block = min(512, total_q)
    q_count = total_q // q_block
    q_blocks = q_cross.reshape(q_count, q_block, HEADS, head_size)
    s_blocks = query_sheets.astype(jnp.bfloat16).reshape(q_count, q_block, -1)
    k_heads = k_cross.reshape(local_rows, HEADS, head_size)
    v_heads = v_cross.reshape(local_rows, HEADS, head_size)

    def block_masked(parts):
        q_part, s_part = parts
        scores = jnp.einsum("qhe,phe->hqp", q_part, k_heads, preferred_element_type=jnp.float32)
        allowed = jnp.dot(s_part, sheet_rows.T, preferred_element_type=jnp.float32) > 0.5
        masked = jnp.where(allowed[None], scores, -1e30)
        return (masked, jnp.max(masked, axis=-1))

    masked_all, local_peak = lax.map(block_masked, (q_blocks, s_blocks))
    peak = lax.pmax(local_peak.astype(jnp.bfloat16), ("band", "tile")).astype(local_peak.dtype)

    def block_sums(parts):
        masked, peak_part = parts
        weights = jnp.exp(masked - peak_part[:, :, None])
        numer_part = jnp.einsum(
            "hqp,phe->qhe",
            weights.astype(jnp.bfloat16),
            v_heads,
            preferred_element_type=jnp.float32,
        )
        return (numer_part.reshape(q_block, width), jnp.sum(weights, axis=-1).T)

    numer, denom = lax.map(block_sums, (masked_all, peak))
    numer = numer.reshape(total_q, width)
    denom = denom.reshape(total_q, HEADS)
    share = total_q // tiles
    numer_tile, denom_tile = (
        lax.psum_scatter(
            numer.astype(jnp.bfloat16), "tile", scatter_dimension=0, tiled=True
        ).astype(jnp.float32),
        lax.psum_scatter(
            denom.astype(jnp.bfloat16), "tile", scatter_dimension=0, tiled=True
        ).astype(jnp.float32),
    )
    numer_tile, denom_tile = (
        lax.psum(numer_tile.astype(jnp.bfloat16), "band").astype(jnp.float32),
        lax.psum(denom_tile.astype(jnp.bfloat16), "band").astype(jnp.float32),
    )
    rows = numer_tile.shape[0]
    attended = (
        (numer_tile.reshape(rows, HEADS, head_size) / denom_tile[:, :, None])
        .reshape(rows, width)
        .astype(jnp.bfloat16)
    )
    tile_index = lax.axis_index("tile")
    own_queries = lax.dynamic_slice_in_dim(queries, tile_index * share, share, 0)
    own_pos = lax.dynamic_slice_in_dim(query_pos, tile_index * share, share, 0)
    cross_out = jnp.dot(attended, cross_proj[3], preferred_element_type=jnp.float32)
    first_state = layer_norm(own_queries.astype(jnp.float32) + cross_out, norm_gain[0]).astype(
        jnp.bfloat16
    )
    self_in = first_state + own_pos
    q_self = (
        jnp.dot(self_in, self_proj[0], preferred_element_type=jnp.float32) * score_scale
    ).astype(jnp.bfloat16)
    k_self = jnp.dot(self_in, self_proj[1], preferred_element_type=jnp.float32).astype(jnp.bfloat16)
    v_self = jnp.dot(first_state, self_proj[2], preferred_element_type=jnp.float32).astype(
        jnp.bfloat16
    )
    k_every, v_every = (
        lax.all_gather(k_self, "tile", axis=0, tiled=True),
        lax.all_gather(v_self, "tile", axis=0, tiled=True),
    )
    self_out = self_attend(q_self, k_every, v_every, head_size)
    second_state = layer_norm(
        first_state.astype(jnp.float32)
        + jnp.dot(self_out, self_proj[3], preferred_element_type=jnp.float32),
        norm_gain[1],
    ).astype(jnp.bfloat16)
    hidden = jnp.maximum(
        jnp.dot(second_state, mlp_in, preferred_element_type=jnp.float32), 0.0
    ).astype(jnp.bfloat16)
    return layer_norm(
        second_state.astype(jnp.float32)
        + jnp.dot(hidden, mlp_out, preferred_element_type=jnp.float32),
        norm_gain[2],
    ).astype(jnp.bfloat16)


def solution(mesh):
    return jax.shard_map(
        body,
        mesh=mesh,
        in_specs=(
            P(),
            P(),
            P(("band", "tile"), None),
            P(("band", "tile")),
            P(("band", "tile")),
            P(),
            P(),
            P(),
            P(),
            P(),
            P(),
            P(),
        ),
        out_specs=P("tile", None),
        check_vma=False,
    )
```

profile of v0, /device:TPU:1, one launch (start us, length us, event | category | flops | bytes accessed | tf_op | source)
XLA Modules:
  0.0 613.5 jit_solution(5391888160078777365)
XLA Ops:
  6.5 5.0 multiply_convert_fusion
  11.6 6.2 %reshape.83 = bf16[4,512,8,64]{3,2,1,0:T(8,128)(2,1)} reshape(bf16[2048,512]{1,0:T(8,128)(2,1)} %multiply_convert_fusion) | data formatting | bytes 4194304 | tf_op jit(solution)/shard_map/reshape | solution.py:73
  17.8 5.5 copy.32
  23.3 1.7 convolution_convert_fusion
  25.0 2.7 convolution_convert_fusion.1
  27.7 30.2 %while.26 = (s32[]{:T(128)}, f32[4,8,512,512]{2,3,1,0:T(8,128)}, bf16[4,8,512]{2,1,0:T(8,128)(2,1)S(1)}, bf16[4,512,16]{1,2,0:T(8,128)(2,1)S(1)}, bf16[4,512,8,6...) while((s32[]{:T(128)}, f32[4,8,512,512]{2,3,1,0:T(8,128)}, ...), condition=%wide.region_2.3_spmd.clone, body=%wide.region_0.2_spmd.clone.sunk | while | flops 285487104 | bytes 19180636 | solution.py:85
  27.7 0.4 convolution_compare_fusion.2
  28.1 0.4 copy.67
  28.5 5.8 bitcast_dynamic-update-slice_fusion.7
  34.3 0.9 select_reduce_fusion.2
  35.3 0.4 convolution_compare_fusion.2
  35.7 0.4 copy.67
  36.1 5.8 bitcast_dynamic-update-slice_fusion.7
  41.9 0.9 select_reduce_fusion.2
  42.8 0.4 convolution_compare_fusion.2
  43.3 0.4 copy.67
  43.7 5.8 bitcast_dynamic-update-slice_fusion.7
  49.5 0.9 select_reduce_fusion.2
  50.4 0.4 convolution_compare_fusion.2
  50.8 0.4 copy.67
  51.2 5.8 bitcast_dynamic-update-slice_fusion.7
  57.0 0.9 select_reduce_fusion.2
  57.9 81.6 %pmax.7 = bf16[4,8,512]{2,1,0:T(8,128)(2,1)S(1)} all-reduce(bf16[4,8,512]{2,1,0:T(8,128)(2,1)S(1)} %get-tuple-element.77), channel_id=1, replica_groups=mesh['band'=8,'tile'=32] {'band','tile'}, use_global_device_ids=true, to_apply=%region_3.4 | all-reduce | flops 16384 | bytes 65536 | tf_op jit(solution)/shard_map/pmax | solution.py:86
  139.6 109.4 %while.25 = (s32[]{:T(128)}, bf16[4,512,512]{2,1,0:T(8,128)(2,1)}, bf16[4,512,8]{1,2,0:T(8,128)(2,1)S(1)}, f32[4,8,512,512]{2,3,1,0:T(8,128)}, f32[4,8,512]{2,1,...) while((s32[]{:T(128)}, bf16[4,512,512]{2,1,0:T(8,128)(2,1)}, bf16[4,512,8]{1,2,0:T(8,128)(2,1)S(1)}, ...), condition=%wide.region_6.7_spmd, body=%wide.region_4.6_spmd.sunk | while | flops 276819968 | bytes 57762448 | solution.py:99
  139.6 7.7 %constant_dynamic-slice_fusion.2 = f32[1,8,512,512]{2,3,1,0:T(8,128)} fusion(f32[4,8,512,512]{2,3,1,0:T(8,128)} %get-tuple-element.302, s32[]{:T(128)} %get-tuple-element.292), kind=kLoop, calls=%fused_computation.10.clone.1 | loop fusion | bytes 16777220 | tf_op jit(solution)/shard_map/while/body/jit(dynamic_index_in_dim)/dynamic_slice | solution.py:99
  147.3 9.1 %copy.65 = f32[1,8,512,512]{3,2,1,0:T(8,128)} copy(f32[1,8,512,512]{2,3,1,0:T(8,128)} %constant_dynamic-slice_fusion.2) | data formatting | bytes 16777216 | tf_op jit(solution)/shard_map/while/body/jit(dynamic_index_in_dim)/dynamic_slice | solution.py:99
  156.5 4.9 fusion.86
  161.6 0.8 constant_dynamic-update-slice_fusion.2
  162.4 4.5 fusion.87
  166.9 7.7 %constant_dynamic-slice_fusion.2 = f32[1,8,512,512]{2,3,1,0:T(8,128)} fusion(f32[4,8,512,512]{2,3,1,0:T(8,128)} %get-tuple-element.302, s32[]{:T(128)} %get-tuple-element.292), kind=kLoop, calls=%fused_computation.10.clone.1 | loop fusion | bytes 16777220 | tf_op jit(solution)/shard_map/while/body/jit(dynamic_index_in_dim)/dynamic_slice | solution.py:99
  174.7 9.1 %copy.65 = f32[1,8,512,512]{3,2,1,0:T(8,128)} copy(f32[1,8,512,512]{2,3,1,0:T(8,128)} %constant_dynamic-slice_fusion.2) | data formatting | bytes 16777216 | tf_op jit(solution)/shard_map/while/body/jit(dynamic_index_in_dim)/dynamic_slice | solution.py:99
  183.8 4.9 fusion.86
  188.9 0.8 constant_dynamic-update-slice_fusion.2
  189.8 4.5 fusion.87
  194.3 7.7 %constant_dynamic-slice_fusion.2 = f32[1,8,512,512]{2,3,1,0:T(8,128)} fusion(f32[4,8,512,512]{2,3,1,0:T(8,128)} %get-tuple-element.302, s32[]{:T(128)} %get-tuple-element.292), kind=kLoop, calls=%fused_computation.10.clone.1 | loop fusion | bytes 16777220 | tf_op jit(solution)/shard_map/while/body/jit(dynamic_index_in_dim)/dynamic_slice | solution.py:99
  202.0 9.1 %copy.65 = f32[1,8,512,512]{3,2,1,0:T(8,128)} copy(f32[1,8,512,512]{2,3,1,0:T(8,128)} %constant_dynamic-slice_fusion.2) | data formatting | bytes 16777216 | tf_op jit(solution)/shard_map/while/body/jit(dynamic_index_in_dim)/dynamic_slice | solution.py:99
  211.2 4.9 fusion.86
  216.3 0.8 constant_dynamic-update-slice_fusion.2
  217.1 4.5 fusion.87
  221.6 7.7 %constant_dynamic-slice_fusion.2 = f32[1,8,512,512]{2,3,1,0:T(8,128)} fusion(f32[4,8,512,512]{2,3,1,0:T(8,128)} %get-tuple-element.302, s32[]{:T(128)} %get-tuple-element.292), kind=kLoop, calls=%fused_computation.10.clone.1 | loop fusion | bytes 16777220 | tf_op jit(solution)/shard_map/while/body/jit(dynamic_index_in_dim)/dynamic_slice | solution.py:99
  229.4 9.1 %copy.65 = f32[1,8,512,512]{3,2,1,0:T(8,128)} copy(f32[1,8,512,512]{2,3,1,0:T(8,128)} %constant_dynamic-slice_fusion.2) | data formatting | bytes 16777216 | tf_op jit(solution)/shard_map/while/body/jit(dynamic_index_in_dim)/dynamic_slice | solution.py:99
  238.5 4.9 fusion.86
  243.4 0.2 copy.66
  243.7 0.8 constant_dynamic-update-slice_fusion.2
  244.5 4.5 fusion.87
  249.1 1.0 copy.41
  250.1 79.2 %reduce-scatter.5.cloned.1.call-done = bf16[64,512]{1,0:T(8,128)(2,1)} async-done(((bf16[2048,512]{1,0:T(8,128)(2,1)}), bf16[64,512]{1,0:T(8,128)(2,1)}) %reduce-scatter.5.cloned.1.call-update) | async-done | bytes 65552 | tf_op jit(solution)/shard_map/reduce_scatter | solution.py:104
  329.4 87.7 %reduce-scatter.7.cloned.1.call-done = bf16[64,8]{1,0:T(8,128)(2,1)} async-done(((bf16[2048,8]{1,0:T(8,128)(2,1)}), bf16[64,8]{1,0:T(8,128)(2,1)}) %reduce-scatter.7.cloned.1.call-update) | async-done | bytes 1040
  417.1 0.8 copy.42
  417.9 13.9 %psum.15 = bf16[64,8]{0,1:T(8,128)(2,1)S(1)} all-reduce(bf16[64,8]{0,1:T(8,128)(2,1)S(1)} %copy.42), channel_id=1, replica_groups=mesh['band'=8,'tile'=32] {'band'}, use_global_device_ids=true, to_apply=%region_10.11 | all-reduce | flops 512 | bytes 2048 | tf_op jit(solution)/shard_map/psum | solution.py:113
  432.1 54.8 %all-reduce.2.cloned.1.call-done = bf16[64,512]{1,0:T(8,128)(2,1)} async-done(((bf16[64,512]{1,0:T(8,128)(2,1)}), bf16[64,512]{1,0:T(8,128)(2,1)}) %all-reduce.2.cloned.1.call-update) | async-done | bytes 65552 | tf_op jit(solution)/shard_map/psum | solution.py:112
  486.9 1.4 fusion.61
  488.6 1.9 convolution_convert_fusion.2
  490.6 1.9 convolution_convert_fusion.3
  492.5 1.3 fusion.26
  493.9 49.5 %all-gather.5.cloned.1.call-done = bf16[2048,512]{1,0:T(8,128)(2,1)} async-done(((bf16[64,512]{1,0:T(8,128)(2,1)}), bf16[2048,512]{1,0:T(8,128)(2,1)}) %all-gather.5.cloned.1.call-update) | async-done | bytes 2097168 | tf_op jit(solution)/shard_map/all_gather | solution.py:137
  543.4 4.0 copy.37
  547.4 4.7 fusion.62
  552.1 42.2 %all-gather.3.cloned.1.call-done = bf16[2048,512]{1,0:T(8,128)(2,1)} async-done(((bf16[64,512]{1,0:T(8,128)(2,1)}), bf16[2048,512]{1,0:T(8,128)(2,1)}) %all-gather.3.cloned.1.call-update) | async-done | bytes 2097168 | tf_op jit(solution)/shard_map/all_gather | solution.py:138
  594.3 4.0 copy.36
  598.3 3.6 fusion.24
  601.9 1.4 fusion.65
  603.5 2.6 fusion.66
  606.3 0.7 multiply_convert_fusion.1
  (75 shorter events, 2.2 us)
Async XLA Ops:
  6.5 596.9 %copy-start = (bf16[2048,512]{1,0:T(8,128)(2,1)S(1)}, bf16[2048,512]{1,0:T(8,128)(2,1)}, u32[]{:S(2)}) copy-start(bf16[2048,512]{1,0:T(8,128)(2,1)} %param.26) | copy-start | bytes 6291460
  6.5 322.8 %reduce-scatter.5.cloned.1.call-start = ((), (), s32[]{:S(2)}) async-start(), calls=%async_computation.2 | async-start | bytes 2162688 | tf_op jit(solution)/shard_map/reduce_scatter | solution.py:104
  17.8 5.5 copy-start.3
  17.8 7.2 %copy-start.5 = (bf16[4,512]{1,0:T(4,128)(2,1)S(1)}, bf16[4,512]{1,0:T(4,128)(2,1)}, u32[]{:S(2)}) copy-start(bf16[4,512]{1,0:T(4,128)(2,1)} %param.22) | copy-start | bytes 12292
  17.8 7.2 %copy-start.6 = (s32[512]{0:T(512)S(1)}, s32[512]{0:T(512)}, u32[]{:S(2)}) copy-start(s32[512]{0:T(512)} %param.19) | copy-start | bytes 6148
  23.2 4.5 copy-start.7
  139.6 16.9 %copy-start.1 = (bf16[512,8,64]{0,2,1:T(8,128)(2,1)}, bf16[512,8,64]{0,2,1:T(8,128)(2,1)S(1)}, u32[]{:S(2)}) copy-start(bf16[512,8,64]{0,2,1:T(8,128)(2,1)S(1)} %get-tuple-element.304) | copy-start | bytes 1572868 | tf_op jit(solution)/shard_map/while
  162.4 4.5 copy-start.2
  166.9 16.9 %copy-start.1 = (bf16[512,8,64]{0,2,1:T(8,128)(2,1)}, bf16[512,8,64]{0,2,1:T(8,128)(2,1)S(1)}, u32[]{:S(2)}) copy-start(bf16[512,8,64]{0,2,1:T(8,128)(2,1)S(1)} %get-tuple-element.304) | copy-start | bytes 1572868 | tf_op jit(solution)/shard_map/while
  189.8 4.5 copy-start.2
  194.3 16.9 %copy-start.1 = (bf16[512,8,64]{0,2,1:T(8,128)(2,1)}, bf16[512,8,64]{0,2,1:T(8,128)(2,1)S(1)}, u32[]{:S(2)}) copy-start(bf16[512,8,64]{0,2,1:T(8,128)(2,1)S(1)} %get-tuple-element.304) | copy-start | bytes 1572868 | tf_op jit(solution)/shard_map/while
  217.1 4.5 copy-start.2
  221.6 16.9 %copy-start.1 = (bf16[512,8,64]{0,2,1:T(8,128)(2,1)}, bf16[512,8,64]{0,2,1:T(8,128)(2,1)S(1)}, u32[]{:S(2)}) copy-start(bf16[512,8,64]{0,2,1:T(8,128)(2,1)S(1)} %get-tuple-element.304) | copy-start | bytes 1572868 | tf_op jit(solution)/shard_map/while
  244.5 4.5 copy-start.2
  249.0 80.4 %copy-start.4 = (f32[3,512]{1,0:T(4,128)S(1)}, f32[3,512]{1,0:T(4,128)}, u32[]{:S(2)}) copy-start(f32[3,512]{1,0:T(4,128)} %param.27) | copy-start | bytes 18436
  249.0 168.0 %reduce-scatter.7.cloned.1.call-start = ((), (), s32[]{:S(2)}) async-start(), calls=%async_computation.6 | async-start | bytes 540672
  250.1 236.8 %all-reduce.2.cloned.1.call-start = ((), (), s32[]{:S(2)}) async-start(), calls=%async_computation.3 | async-start | bytes 131072 | tf_op jit(solution)/shard_map/psum | solution.py:112
  329.3 214.0 %all-gather.5.cloned.1.call-start = ((), (), s32[]{:S(2)}) async-start(), calls=%async_computation.5 | async-start | bytes 2162688 | tf_op jit(solution)/shard_map/all_gather | solution.py:137
  490.5 103.7 %all-gather.3.cloned.1.call-start = ((), (), s32[]{:S(2)}) async-start(), calls=%async_computation.4 | async-start | bytes 2162688 | tf_op jit(solution)/shard_map/all_gather | solution.py:138
Sparse Core Ops, SparseCore 0:
  249.1 80.1 reduce-scatter.4
  333.0 83.9 reduce-scatter.6
  419.4 67.4 all-reduce.1
  490.6 52.6 all-gather.4
  546.1 48.1 all-gather.2
where the time goes:
time: 615 us; the launch traced here: 614 us
  waiting for transfers between devices  313 us (51%)
  blocking collectives  95.5 us (16%)
  local copies, waits for them, and re-layouts  95.3 us (15%)
  matrix products  72.7 us (12%)
  other arithmetic  22.9 us (4%)
  between operations  13.3 us (2%)
    unnamed x6, waiting for transfers between devices  87.7 us
    pmax x1, blocking collectives, body(): lax.pmax(local_peak.astype(jnp.bfloat16), ('band', 'tile'))  81.6 us
    reduce_scatter x1, waiting for transfers between devices, body(): lax.psum_scatter(numer.astype(jnp.bfloat16), 'tile', scatter_dimension=0,...  79.2 us
    dynamic_slice x8, local copies, waits for them, and re-layouts, body(): numer, denom = lax.map(block_sums, (masked_all, peak))  67.4 us
    psum x1, waiting for transfers between devices, body(): lax.psum(numer_tile.astype(jnp.bfloat16), 'band').astype(jnp.float32)  54.8 us
    all_gather x1, waiting for transfers between devices, body(): lax.all_gather(k_self, 'tile', axis=0, tiled=True)  49.5 us
    all_gather x1, waiting for transfers between devices, body(): lax.all_gather(v_self, 'tile', axis=0, tiled=True)  42.2 us
    dot_general x4, matrix products, block_masked(): jnp.einsum('qhe,phe->hqp', q_part, k_heads, preferred_element_type=jnp.fl...  23.2 us
  transfers between devices with their start and end apart: 5, of which 5 were waited for; matrix products, arithmetic and copies ran while one was open for 2% of the time, Pallas kernels for 0%

commit v1 on v0

v1 whole, which is shorter than its diff:
```python
import functools
import math

import jax
import jax.numpy as jnp
import numpy as np
from jax import lax
from jax.experimental import pallas as pl
from jax.experimental.pallas import tpu as pltpu
from jax.sharding import Mesh
from jax.sharding import PartitionSpec as P

HEADS = 8
LANES = 128
NEG = -1e30
NT = (((1,), (1,)), ((), ()))
F32 = jnp.float32
BF16 = jnp.bfloat16


def layer_norm(values, gain):
    center = jnp.mean(values, axis=-1, keepdims=True)
    shifted = values - center
    spread = jnp.mean(shifted * shifted, axis=-1, keepdims=True)
    return shifted * lax.rsqrt(spread + 1e-05) * gain


def pack_stats(peak, total):
    hi = peak.astype(BF16).astype(F32)
    rest = peak - hi
    mid = rest.astype(BF16).astype(F32)
    low = rest - mid
    total_hi = total.astype(BF16).astype(F32)
    total_low = total - total_hi
    group = lax.broadcasted_iota(jnp.int32, peak.shape, 1) // HEADS
    packed = jnp.where(
        group == 0,
        hi,
        jnp.where(
            group == 1,
            mid,
            jnp.where(group == 2, low, jnp.where(group == 3, total_hi, total_low)),
        ),
    )
    return jnp.where(group < 5, packed, 0.0).astype(BF16)


def spread_matrices(width):
    lane = np.arange(LANES)
    columns = np.arange(width + LANES)
    head = np.where(columns < width, columns // (width // HEADS), (columns - width) % HEADS)
    same = (lane[:, None] % HEADS) == head[None, :]
    group = lane[:, None] // HEADS
    peak = same & (group < 3)
    total = same & (group >= 3) & (group < 5)
    return jnp.asarray(peak, BF16), jnp.asarray(total, BF16)


def cross_kernel(
    core_ref,
    queries_ref,
    pos_ref,
    sheets_ref,
    own_ref,
    other_ref,
    own_id_ref,
    other_id_ref,
    level_ref,
    proj_ref,
    out_ref,
    keys,
    values,
    bias,
):
    width = own_ref.shape[1]
    head_size = width // HEADS
    half = own_ref.shape[0]
    levels = level_ref.shape[0]
    pairs = width // LANES

    @pl.when(pl.program_id(0) == 0)
    def _():
        bias[...] = jnp.zeros(bias.shape, bias.dtype)
        lane = lax.broadcasted_iota(jnp.int32, (half, LANES), 1)
        for part, (patch, ids) in enumerate(((own_ref, own_id_ref), (other_ref, other_id_ref))):
            rows = pl.ds(part * half, half)
            columns = ids[...].astype(F32)
            level = jnp.transpose(jnp.broadcast_to(columns[0:1], (LANES, half)))
            sheet = jnp.transpose(jnp.broadcast_to(columns[1:2], (LANES, half)))
            patches = patch[...]
            level = jnp.concatenate([level] * pairs, axis=1)
            added = jnp.zeros((half, width), F32)
            for index in range(levels):
                row = level_ref[index : index + 1].astype(F32)
                added = jnp.where(level == float(index), row, added)
            key_input = (patches.astype(F32) + added).astype(BF16)
            k_all = jnp.dot(key_input, proj_ref[1], preferred_element_type=F32).astype(BF16)
            v_all = jnp.dot(patches, proj_ref[2], preferred_element_type=F32).astype(BF16)
            on_sheet = (sheet == lane.astype(F32)).astype(BF16)
            for head in range(HEADS):
                cut = slice(head // 2 * LANES, head // 2 * LANES + LANES)
                inside = (lane // head_size) == (head % 2)
                keys[head, rows, :LANES] = jnp.where(inside, k_all[:, cut], 0)
                keys[head, rows, LANES:] = on_sheet
                values[head, rows, :LANES] = jnp.where(inside, v_all[:, cut], 0)
                values[head, rows, LANES:] = (lane % HEADS == head).astype(BF16)

    block = queries_ref.shape[0] * queries_ref.shape[1]
    mixed = queries_ref[...].reshape(block, width) + pos_ref[...].reshape(block, width)
    scale = math.log2(math.e) / math.sqrt(head_size)
    q_all = (jnp.dot(mixed, proj_ref[0], preferred_element_type=F32) * scale).astype(BF16)
    sheets = sheets_ref[...].reshape(block, sheets_ref.shape[2])
    bias[:, : sheets_ref.shape[2]] = jnp.where(sheets == 1, 0.0, NEG).astype(BF16)
    barred = bias[...]
    lane = lax.broadcasted_iota(jnp.int32, (block, LANES), 1)
    peaks = jnp.zeros((block, LANES), F32)
    totals = jnp.zeros((block, LANES), F32)
    shape = (out_ref.shape[0], out_ref.shape[1], LANES)
    for pair in range(pairs):
        cut = slice(pair * LANES, pair * LANES + LANES)
        left = jnp.concatenate([q_all[:, cut], barred], axis=1)
        sums = jnp.zeros((block, 2 * LANES), F32)
        for head in (2 * pair, 2 * pair + 1):
            scores = lax.dot_general(left, keys[head], NT, preferred_element_type=F32)
            peak = jnp.max(scores, axis=1, keepdims=True)
            weights = jnp.exp2(scores - peak).astype(BF16)
            sums += jnp.dot(weights, values[head], preferred_element_type=F32)
            peaks = jnp.where(lane % HEADS == head, peak, peaks)
        out_ref[:, :, cut] = sums[:, :LANES].astype(BF16).reshape(shape)
        totals += sums[:, LANES:]
    out_ref[:, :, width:] = pack_stats(peaks, totals).reshape(shape)


def cross_partial(core, queries, query_pos, query_sheets, own, other, own_ids, other_ids, level, proj):
    total, width = queries.shape
    rows = 64
    groups = total // (2 * rows)
    step = 4
    half = own.shape[0]
    sheets = query_sheets.shape[1]
    view = lambda array: array.reshape(groups, 2, rows, array.shape[1])
    by_core = lambda last: pl.BlockSpec(
        (step, None, rows, last), lambda i, core_ref: (i, core_ref[0], 0, 0)
    )
    whole = lambda shape: pl.BlockSpec(shape, lambda i, core_ref: (0,) * len(shape))
    return pl.pallas_call(
        cross_kernel,
        grid_spec=pltpu.PrefetchScalarGridSpec(
            num_scalar_prefetch=1,
            grid=(groups // step,),
            in_specs=[
                by_core(width),
                by_core(width),
                by_core(sheets),
                whole((half, width)),
                whole((half, width)),
                whole((2, half)),
                whole((2, half)),
                whole(level.shape),
                whole((3, width, width)),
            ],
            out_specs=pl.BlockSpec((step, rows, width + LANES), lambda i, core_ref: (i, 0, 0)),
            scratch_shapes=[
                pltpu.VMEM((HEADS, 2 * half, 2 * LANES), BF16),
                pltpu.VMEM((HEADS, 2 * half, 2 * LANES), BF16),
                pltpu.VMEM((step * rows, LANES), BF16),
            ],
        ),
        out_shape=jax.ShapeDtypeStruct((groups, rows, width + LANES), BF16),
        compiler_params=pltpu.CompilerParams(vmem_limit_bytes=48 * 2**20),
        name="cross_partial",
    )(core, view(queries), view(query_pos), view(query_sheets), own, other, own_ids, other_ids, level, proj)


def combine(parts_ref, peak_matrix, total_matrix):
    count, rows, full = parts_ref.shape
    width = full - LANES
    stats = [parts_ref[i, :, width:] for i in range(count)]
    peaks = [jnp.dot(s, peak_matrix, preferred_element_type=F32) for s in stats]
    top = functools.reduce(jnp.maximum, peaks)
    sums = jnp.zeros((rows, width), F32)
    total = jnp.zeros((rows, full), F32)
    for i in range(count):
        factor = jnp.exp2(peaks[i] - top)
        sums += factor[:, :width] * parts_ref[i, :, :width].astype(F32)
        total += factor * jnp.dot(stats[i], total_matrix, preferred_element_type=F32)
    return sums, top, total


def merge_kernel(parts_ref, peak_ref, total_ref, out_ref):
    sums, top, total = combine(parts_ref, peak_ref[...], total_ref[...])
    width = sums.shape[1]
    sums = sums.astype(BF16)
    stats = pack_stats(top[:, width:], total[:, width:])
    for i in range(out_ref.shape[0]):
        out_ref[i, :, :width] = sums
        out_ref[i, :, width:] = stats


def merge(parts, peak_matrix, total_matrix, copies):
    return pl.pallas_call(
        merge_kernel,
        out_shape=jax.ShapeDtypeStruct((copies,) + parts.shape[1:], BF16),
        compiler_params=pltpu.CompilerParams(vmem_limit_bytes=32 * 2**20),
        name="merge",
    )(parts, peak_matrix, total_matrix)


def first_kernel(tile_ref, parts_ref, peak_ref, total_ref, queries_ref, proj_ref, gain_ref, out_ref):
    sums, _, total = combine(parts_ref, peak_ref[...], total_ref[...])
    attended = (sums / total[:, : sums.shape[1]]).astype(BF16)
    crossed = jnp.dot(attended, proj_ref[...], preferred_element_type=F32)
    first = layer_norm(queries_ref[...].astype(F32) + crossed, gain_ref[0:1]).astype(BF16)
    for i in range(out_ref.shape[0]):
        out_ref[i] = first


def first_state_of(tile, parts, peak_matrix, total_matrix, queries, proj, gain, copies):
    _, rows, full = parts.shape
    width = full - LANES
    whole = lambda shape: pl.BlockSpec(shape, lambda i, tile_ref: (0,) * len(shape))
    return pl.pallas_call(
        first_kernel,
        grid_spec=pltpu.PrefetchScalarGridSpec(
            num_scalar_prefetch=1,
            grid=(1,),
            in_specs=[
                whole(parts.shape),
                whole(peak_matrix.shape),
                whole(total_matrix.shape),
                pl.BlockSpec((rows, width), lambda i, tile_ref: (tile_ref[0], 0)),
                pl.BlockSpec((None, width, width), lambda i, tile_ref: (3, 0, 0)),
                whole(gain.shape),
            ],
            out_specs=pl.BlockSpec((copies, rows, width), lambda i, tile_ref: (0, 0, 0)),
        ),
        out_shape=jax.ShapeDtypeStruct((copies, rows, width), BF16),
        compiler_params=pltpu.CompilerParams(vmem_limit_bytes=32 * 2**20),
        name="first_state",
    )(tile, parts, peak_matrix, total_matrix, queries, proj, gain)


def tail_kernel(
    place_ref,
    first_ref,
    own_pos_ref,
    own_ref,
    other_ref,
    pos_a_ref,
    pos_b_ref,
    proj_ref,
    mlp_in_ref,
    mlp_out_ref,
    gain_ref,
    out_ref,
):
    rows, width = first_ref.shape
    head_size = width // HEADS
    keys = own_ref.shape[0] * own_ref.shape[1]
    first = first_ref[...]
    scale = math.log2(math.e) / math.sqrt(head_size)
    q_self = jnp.dot(first + own_pos_ref[...], proj_ref[0], preferred_element_type=F32) * scale
    q_self = q_self.astype(BF16)
    stacked = jnp.concatenate([q_self] * HEADS, axis=0)
    row_head = lax.broadcasted_iota(jnp.int32, stacked.shape, 0) // rows
    col_head = lax.broadcasted_iota(jnp.int32, stacked.shape, 1) // head_size
    mine = row_head == col_head
    stacked = jnp.where(mine, stacked, 0)
    absorbed = lax.dot_general(stacked, proj_ref[1], NT, preferred_element_type=F32).astype(BF16)
    states = [ref[...].reshape(keys, width) for ref in (own_ref, other_ref)]
    inputs = [
        state + ref[...].reshape(keys, width) for state, ref in zip(states, (pos_a_ref, pos_b_ref))
    ]
    scores = [lax.dot_general(absorbed, x, NT, preferred_element_type=F32) for x in inputs]
    peak = functools.reduce(jnp.maximum, [jnp.max(s, axis=1, keepdims=True) for s in scores])
    weights = [jnp.exp2(s - peak) for s in scores]
    total = sum(jnp.sum(w, axis=1, keepdims=True) for w in weights)
    mixed = sum(
        jnp.dot(w.astype(BF16), state, preferred_element_type=F32)
        for w, state in zip(weights, states)
    )
    mixed = (mixed / total).astype(BF16)
    blended = jnp.dot(mixed, proj_ref[2], preferred_element_type=F32)
    blended = jnp.where(mine, blended, 0.0)
    self_out = sum(blended[h * rows : (h + 1) * rows] for h in range(HEADS)).astype(BF16)
    second = first.astype(F32) + jnp.dot(self_out, proj_ref[3], preferred_element_type=F32)
    second = layer_norm(second, gain_ref[1:2]).astype(BF16)
    hidden = jnp.dot(second, mlp_in_ref[...], preferred_element_type=F32)
    hidden = jnp.maximum(hidden, 0.0).astype(BF16)
    decoded = second.astype(F32) + jnp.dot(hidden, mlp_out_ref[...], preferred_element_type=F32)
    out_ref[...] = layer_norm(decoded, gain_ref[2:3]).astype(BF16)


def tail(place, first, own, other, query_pos, proj, mlp_in, mlp_out, gain):
    groups, rows, width = own.shape
    pos = query_pos.reshape(groups, 2, rows, width)
    whole = lambda shape: pl.BlockSpec(shape, lambda i, place_ref: (0,) * len(shape))
    return pl.pallas_call(
        tail_kernel,
        grid_spec=pltpu.PrefetchScalarGridSpec(
            num_scalar_prefetch=1,
            grid=(1,),
            in_specs=[
                pl.BlockSpec((None, rows, width), lambda i, place_ref: (0, 0, 0)),
                pl.BlockSpec((rows, width), lambda i, place_ref: (place_ref[1], 0)),
                whole(own.shape),
                whole(other.shape),
                pl.BlockSpec((groups, None, rows, width), lambda i, place_ref: (0, place_ref[0], 0, 0)),
                pl.BlockSpec(
                    (groups, None, rows, width), lambda i, place_ref: (0, 1 - place_ref[0], 0, 0)
                ),
                whole(proj.shape),
                whole(mlp_in.shape),
                whole(mlp_out.shape),
                whole(gain.shape),
            ],
            out_specs=pl.BlockSpec((rows, width), lambda i, place_ref: (0, 0)),
        ),
        out_shape=jax.ShapeDtypeStruct((rows, width), BF16),
        compiler_params=pltpu.CompilerParams(vmem_limit_bytes=56 * 2**20),
        name="tail",
    )(place, first, query_pos, own, other, pos, pos, proj, mlp_in, mlp_out, gain)


def body(
    queries,
    query_pos,
    patches,
    patch_level,
    patch_sheet,
    query_sheets,
    level_embed,
    cross_proj,
    self_proj,
    mlp_in,
    mlp_out,
    norm_gain,
):
    core = lax.axis_index("c").astype(jnp.int32)
    square = lax.axis_size("x") * lax.axis_size("y")
    bands = lax.axis_size("z")
    tile = (lax.axis_index("x") * lax.axis_size("y") + lax.axis_index("y")) * 2 + core
    place = jnp.stack([core, tile.astype(jnp.int32)])
    swap = [(0, 1), (1, 0)]
    ids = jnp.stack([patch_level, patch_sheet])
    other_patches = lax.ppermute(patches, "c", swap)
    other_ids = lax.ppermute(ids, "c", swap)
    peak_matrix, total_matrix = spread_matrices(queries.shape[1])
    parts = cross_partial(
        place,
        queries,
        query_pos,
        query_sheets,
        patches,
        other_patches,
        ids,
        other_ids,
        level_embed,
        cross_proj[:3],
    )
    parts = lax.all_to_all(parts, ("x", "y"), 0, 0, tiled=True)
    parts = merge(parts, peak_matrix, total_matrix, bands)
    parts = lax.all_to_all(parts, "z", 0, 0, tiled=True)
    first = first_state_of(
        place[1:], parts, peak_matrix, total_matrix, queries, cross_proj, norm_gain, square
    )
    own = lax.all_to_all(first, ("x", "y"), 0, 0, tiled=True)
    other = lax.ppermute(own, "c", swap)
    return tail(place, first, own, other, query_pos, self_proj, mlp_in, mlp_out, norm_gain)


def solution(mesh):
    devices = mesh.devices
    grid = Mesh(devices.reshape(devices.shape[0], 4, 4, 2), ("z", "x", "y", "c"))
    every = ("z", "x", "y", "c")
    return jax.shard_map(
        body,
        mesh=grid,
        in_specs=(
            P(),
            P(),
            P(every, None),
            P(every),
            P(every),
            P(),
            P(),
            P(),
            P(),
            P(),
            P(),
            P(),
        ),
        out_specs=P(("x", "y", "c"), None),
        check_vma=False,
    )
```

time: 615 us -> 111 us (0.18)
  waiting for transfers between devices: 313 us -> 2.29 us
  local copies, waits for them, and re-layouts: 95.3 us -> 3.82 us
  matrix products: 72.7 us -> 0 us
  blocking collectives: 95.5 us -> 64.5 us
  Pallas kernels: 0 us -> 29.4 us
  other arithmetic: 22.9 us -> 0.78 us
  between operations: 13.3 us -> 0.14 us
  starting transfers between devices: 0.17 us -> 9.49 us
    all_gather x2 -> x0, waiting for transfers between devices: 91.7 us -> none  [the longest x1 49.5 us: body(): lax.all_gather(k_self, 'tile', axis=0, tiled=True)]
    unnamed x6 -> x0, waiting for transfers between devices: 87.7 us -> none
    pmax x1 -> x0, blocking collectives: 81.6 us -> none  [body(): lax.pmax(local_peak.astype(jnp.bfloat16), ('band', 'tile'))]
    reduce_scatter x1 -> x0, waiting for transfers between devices: 79.2 us -> none  [body(): lax.psum_scatter(numer.astype(jnp.bfloat16), 'tile', scatter_dimension=0,...]
    dot_general x22 -> x0, matrix products: 68 us -> none  [the longest x4 23.2 us: block_masked(): jnp.einsum('qhe,phe->hqp', q_part, k_heads, preferred_element_type=jnp.fl...]
    dynamic_slice x8 -> x0, local copies, waits for them, and re-layouts: 67.4 us -> none  [body(): numer, denom = lax.map(block_sums, (masked_all, peak))]
    all_to_all x0 -> x3, blocking collectives: none -> 64.5 us  [the longest x1 25.2 us: body(): parts = lax.all_to_all(parts, 'z', 0, 0, tiled=True)]
    psum x1 -> x0, waiting for transfers between devices: 54.8 us -> none  [body(): lax.psum(numer_tile.astype(jnp.bfloat16), 'band').astype(jnp.float32)]
  transfers between devices with their start and end apart: 5 -> 3, of which waited for: 5 -> 1; matrix products, arithmetic and copies ran while one was open for 2% -> 3% of each run, Pallas kernels for 0% -> 0%
where the time goes in v1:
time: 111 us; the launch traced here: 110 us
  blocking collectives  64.5 us (58%)
  Pallas kernels  29.4 us (26%)
  starting transfers between devices  9.49 us (9%)
  local copies, waits for them, and re-layouts  3.82 us (3%)
  waiting for transfers between devices  2.29 us (2%)
    all_to_all x1, blocking collectives, body(): parts = lax.all_to_all(parts, 'z', 0, 0, tiled=True)  25.2 us
    all_to_all x1, blocking collectives, body(): parts = lax.all_to_all(parts, ('x', 'y'), 0, 0, tiled=True)  23.7 us
    pallas_call x1, Pallas kernels, cross_partial(): pl.pallas_call(cross_kernel, grid_spec=pltpu.PrefetchScalarGridSpec(num_s...  17.2 us
    all_to_all x1, blocking collectives, body(): own = lax.all_to_all(first, ('x', 'y'), 0, 0, tiled=True)  15.5 us
    pallas_call x1, Pallas kernels, tail(): pl.pallas_call(tail_kernel, grid_spec=pltpu.PrefetchScalarGridSpec(num_sc...  10.2 us
    ppermute x1, starting transfers between devices, body(): other = lax.ppermute(own, 'c', swap)  6.25 us
    ppermute x1, starting transfers between devices, body(): other_patches = lax.ppermute(patches, 'c', swap)  3.24 us
    unnamed x23, local copies, waits for them, and re-layouts  2.31 us
  transfers between devices with their start and end apart: 3, of which 1 were waited for; matrix products, arithmetic and copies ran while one was open for 3% of the time, Pallas kernels for 0%

profile of v1, /device:TPU:1, one launch (start us, length us, event | category | flops | bytes accessed | tf_op | source)
XLA Modules:
  0.0 110.4 jit_solution(9887425727178918603)
XLA Ops:
  0.0 3.2 %collective-permute-start = (bf16[512,512]{1,0:T(8,128)(2,1)}, bf16[512,512]{1,0:T(8,128)(2,1)S(1)}, u32[]{:S(2)}, u32[]{:S(2)}) collective-permute-start(bf16[512,512]{1,0:T(8,128)(2,1)} %own_ref.1), channel_id=1, source_target_pairs={{0,1},{1,0},{2,3},{3,2},{4,5},{5,4},{6,7},{7,6},{8,9},{9,8},{10,11... | collective-permute-start | bytes 1572872 | tf_op jit(solution)/shard_map/ppermute | solution.py:346
  3.2 0.7 pad_add_fusion.own_id_ref
  3.9 0.0 collective-permute-start.1
  4.0 0.1 pad_add_fusion.1.core_ref.place_ref
  4.0 0.0 copy-start.8
  4.0 0.0 copy-start.5
  4.0 0.0 copy-start.7
  4.0 1.3 %copy.15 = s32[2048,16]{1,0:T(8,128)S(1)} copy(s32[2048,16]{0,1:T(8,128)} %param.19) | data formatting | bytes 262144 | tf_op args[5]
  5.3 1.5 %slice.3.proj_ref = bf16[3,512,512]{2,1,0:T(8,128)(2,1)S(1)} slice(bf16[4,512,512]{2,1,0:T(8,128)(2,1)} %proj_ref.2), slice={[0:3], [0:512], [0:512]} | slice | bytes 3145728 | tf_op jit(solution)/shard_map/slice | solution.py:359
  6.9 0.0 collective-permute-done.1.other_id_ref
  6.9 0.0 collective-permute-done.other_ref
  6.9 0.0 copy-done.8
  6.9 0.0 copy-done.5
  6.9 0.0 copy-done.7
  6.9 17.2 %cross_partial.1 = bf16[16,64,640]{2,1,0:T(8,128)(2,1)S(1)} custom-call(s32[2]{0:T(128)S(1)} %pad_add_fusion.1.core_ref.place_ref, bf16[16,2,64,512]{3,2,1,0:T(8,128)(2,1)} %bitcast.7, bf16[16,2,64,512]{3,2,1,0:T(8,128)(2,1)} %bitcast.9, s32[16,2,64,16]{3,2,1,0:T(8,128)S(1)} %bitcast.8, bf16[512,512]{1,0:T(8,128)(2,1)S(1)} %copy-done.5, ...), custom_call_target="tpu_custom_call" | custom-call | tf_op jit(solution)/shard_map/cross_partial/pallas_call | solution.py:146
  24.1 0.0 copy-start.3
  24.1 0.0 copy-start.4
  24.1 0.0 copy-start.2
  24.1 23.7 %all_to_all.15.parts_ref = bf16[16,64,640]{2,1,0:T(8,128)(2,1)S(1)} all-to-all(bf16[16,64,640]{2,1,0:T(8,128)(2,1)S(1)} %cross_partial.1), channel_id=1, replica_groups=mesh['z'=8,'x'=4,'y'=4,'c'=2] {'x','y'}, dimensions={0} | all-to-all | bytes 2621440 | tf_op jit(solution)/shard_map/all_to_all | solution.py:361
  47.8 0.0 copy-done.3
  47.8 0.0 copy-done.4
  47.8 0.0 copy-start.1
  47.8 0.0 copy-start.6
  47.9 1.0 merge.1
  48.9 25.2 %all_to_all.16.parts_ref = bf16[8,64,640]{2,1,0:T(8,128)(2,1)S(1)} all-to-all(bf16[8,64,640]{2,1,0:T(8,128)(2,1)S(1)} %merge.1), channel_id=1, replica_groups=mesh['z'=8,'x'=4,'y'=4,'c'=2] {'z'}, dimensions={0} | all-to-all | bytes 1310720 | tf_op jit(solution)/shard_map/all_to_all | solution.py:363
  74.1 0.0 copy-done.2
  74.1 0.0 copy-done.1
  74.1 0.0 copy-done.6
  74.1 1.0 first_state.1.first_ref
  75.1 0.0 copy-start
  75.1 15.5 %all_to_all.17.own_ref = bf16[16,64,512]{2,1,0:T(8,128)(2,1)S(1)} all-to-all(bf16[16,64,512]{2,1,0:T(8,128)(2,1)S(1)} %first_state.1.first_ref), channel_id=1, replica_groups=mesh['z'=8,'x'=4,'y'=4,'c'=2] {'x','y'}, dimensions={0} | all-to-all | bytes 2097152 | tf_op jit(solution)/shard_map/all_to_all | solution.py:367
  90.6 0.0 copy-start.9
  90.6 6.2 %collective-permute-start.2 = (bf16[16,64,512]{2,1,0:T(8,128)(2,1)S(1)}, bf16[16,64,512]{2,1,0:T(8,128)(2,1)S(1)}, u32[]{:S(2)}, u32[]{:S(2)}) collective-permute-start(bf16[16,64,512]{2,1,0:T(8,128)(2,1)S(1)} %all_to_all.17.own_ref), channel_id=1, source_target_pairs={{0,1},{1,0},{2,3},{3,2},{4,5},{5,4},{6,7},{7,6},{8,9},{9,8},{10,11... | collective-permute-start | bytes 3145736 | tf_op jit(solution)/shard_map/ppermute | solution.py:368
  96.9 2.3 %collective-permute-done.2.other_ref = bf16[16,64,512]{2,1,0:T(8,128)(2,1)S(1)} collective-permute-done((bf16[16,64,512]{2,1,0:T(8,128)(2,1)S(1)}, bf16[16,64,512]{2,1,0:T(8,128)(2,1)S(1)}, u32[]{:S(2)}, u32[]{:S(2)}) %collective-permute-start.2) | collective-permute-done | bytes 1048608 | tf_op jit(solution)/shard_map/ppermute | solution.py:368
  99.2 0.0 copy-done
  99.2 0.0 copy-done.9
  99.2 0.0 copy-start.10
  99.2 1.0 copy-done.10
  100.2 10.2 %tail.1 = bf16[64,512]{1,0:T(8,128)(2,1)} custom-call(s32[2]{0:T(128)} %copy-done.8, bf16[16,64,512]{2,1,0:T(8,128)(2,1)} %copy-done, bf16[2048,512]{1,0:T(8,128)(2,1)} %own_pos_ref.1, bf16[16,64,512]{2,1,0:T(8,128)(2,1)} %copy-done.9, bf16[16,64,512]{2,1,0:T(8,128)(2,1)} %copy-done.10, bf16[16,2,64,512]{3,2,1,0:T(8,128)(2,1)} %bitcast.10, ...), custom_call_target="tpu_custom_call" | custom-call | tf_op jit(solution)/shard_map/tail/pallas_call | solution.py:298
Async XLA Ops:
  0.0 6.9 %collective-permute-start = (bf16[512,512]{1,0:T(8,128)(2,1)}, bf16[512,512]{1,0:T(8,128)(2,1)S(1)}, u32[]{:S(2)}, u32[]{:S(2)}) collective-permute-start(bf16[512,512]{1,0:T(8,128)(2,1)} %own_ref.1), channel_id=1, source_target_pairs={{0,1},{1,0},{2,3},{3,2},{4,5},{5,4},{6,7},{7,6},{8,9},{9,8},{10,11... | collective-permute-start | bytes 1572872 | tf_op jit(solution)/shard_map/ppermute | solution.py:346
  3.9 2.9 %collective-permute-start.1 = (s32[2,512]{1,0:T(2,128)S(1)}, s32[2,512]{1,0:T(2,128)S(1)}, u32[]{:S(2)}, u32[]{:S(2)}) collective-permute-start(s32[2,512]{1,0:T(2,128)S(1)} %pad_add_fusion.own_id_ref), channel_id=1, source_target_pairs={{0,1},{1,0},{2,3},{3,2},{4,5},{5,4},{6,7},{7,6},{8,9},{9,8},{10,11... | collective-permute-start | bytes 12296 | tf_op jit(solution)/shard_map/ppermute | solution.py:347
  4.0 2.8 %copy-start.8 = (s32[2]{0:T(128)}, s32[2]{0:T(128)S(1)}, u32[]{:S(2)}) copy-start(s32[2]{0:T(128)S(1)} %pad_add_fusion.1.core_ref.place_ref) | copy-start | bytes 28
  4.0 2.9 %copy-start.5 = (bf16[512,512]{1,0:T(8,128)(2,1)S(1)}, bf16[512,512]{1,0:T(8,128)(2,1)}, u32[]{:S(2)}) copy-start(bf16[512,512]{1,0:T(8,128)(2,1)} %own_ref.1) | copy-start | bytes 1572868
  4.0 2.9 %copy-start.7 = (bf16[4,512]{1,0:T(4,128)(2,1)S(1)}, bf16[4,512]{1,0:T(4,128)(2,1)}, u32[]{:S(2)}) copy-start(bf16[4,512]{1,0:T(4,128)(2,1)} %level_ref.1) | copy-start | bytes 12292
  24.1 23.7 %copy-start.3 = (bf16[128,640]{1,0:T(8,128)(2,1)S(1)}, bf16[128,640]{1,0:T(8,128)(2,1)}, u32[]{:S(2)}) copy-start(bf16[128,640]{1,0:T(8,128)(2,1)} %constant.20.clone.total_ref) | copy-start | bytes 491524
  24.1 23.7 %copy-start.4 = (bf16[128,640]{1,0:T(8,128)(2,1)S(1)}, bf16[128,640]{1,0:T(8,128)(2,1)}, u32[]{:S(2)}) copy-start(bf16[128,640]{1,0:T(8,128)(2,1)} %constant.19.clone.peak_ref) | copy-start | bytes 491524
  24.1 50.0 %copy-start.2 = (bf16[4,512,512]{2,1,0:T(8,128)(2,1)S(1)}, bf16[4,512,512]{2,1,0:T(8,128)(2,1)}, u32[]{:S(2)}) copy-start(bf16[4,512,512]{2,1,0:T(8,128)(2,1)} %proj_ref.2) | copy-start | bytes 6291460
  47.8 26.3 %copy-start.1 = (bf16[2048,512]{1,0:T(8,128)(2,1)S(1)}, bf16[2048,512]{1,0:T(8,128)(2,1)}, u32[]{:S(2)}) copy-start(bf16[2048,512]{1,0:T(8,128)(2,1)} %queries_ref.1) | copy-start | bytes 6291460
  47.8 26.3 %copy-start.6 = (f32[3,512]{1,0:T(4,128)S(1)}, f32[3,512]{1,0:T(4,128)}, u32[]{:S(2)}) copy-start(f32[3,512]{1,0:T(4,128)} %gain_ref.3) | copy-start | bytes 18436
  75.1 24.1 %copy-start = (bf16[16,64,512]{2,1,0:T(8,128)(2,1)}, bf16[16,64,512]{2,1,0:T(8,128)(2,1)S(1)}, u32[]{:S(2)}) copy-start(bf16[16,64,512]{2,1,0:T(8,128)(2,1)S(1)} %first_state.1.first_ref) | copy-start | bytes 3145732
  90.6 8.5 %copy-start.9 = (bf16[16,64,512]{2,1,0:T(8,128)(2,1)}, bf16[16,64,512]{2,1,0:T(8,128)(2,1)S(1)}, u32[]{:S(2)}) copy-start(bf16[16,64,512]{2,1,0:T(8,128)(2,1)S(1)} %all_to_all.17.own_ref) | copy-start | bytes 3145732
  90.6 8.5 %collective-permute-start.2 = (bf16[16,64,512]{2,1,0:T(8,128)(2,1)S(1)}, bf16[16,64,512]{2,1,0:T(8,128)(2,1)S(1)}, u32[]{:S(2)}, u32[]{:S(2)}) collective-permute-start(bf16[16,64,512]{2,1,0:T(8,128)(2,1)S(1)} %all_to_all.17.own_ref), channel_id=1, source_target_pairs={{0,1},{1,0},{2,3},{3,2},{4,5},{5,4},{6,7},{7,6},{8,9},{9,8},{10,11... | collective-permute-start | bytes 3145736 | tf_op jit(solution)/shard_map/ppermute | solution.py:368
  99.2 1.0 copy-start.10

commit v2 on v0

v2 whole, which is shorter than its diff:
```python
import functools
import math

import jax
import jax.numpy as jnp
import numpy as np
from jax import lax
from jax.experimental import pallas as pl
from jax.experimental.pallas import tpu as pltpu
from jax.sharding import Mesh
from jax.sharding import PartitionSpec as P

HEADS = 8
LANES = 128
NEG = -1e30
SMALL = 32 * 2**20
LARGE = 60 * 2**20
NT = (((1,), (1,)), ((), ()))
F32 = jnp.float32
BF16 = jnp.bfloat16


def layer_norm(values, gain):
    center = jnp.mean(values, axis=-1, keepdims=True)
    shifted = values - center
    spread = jnp.mean(shifted * shifted, axis=-1, keepdims=True)
    return shifted * lax.rsqrt(spread + 1e-05) * gain


def pack_stats(peak, total):
    hi = peak.astype(BF16).astype(F32)
    rest = peak - hi
    mid = rest.astype(BF16).astype(F32)
    low = rest - mid
    total_hi = total.astype(BF16).astype(F32)
    total_low = total - total_hi
    group = lax.broadcasted_iota(jnp.int32, peak.shape, 1) // HEADS
    packed = jnp.where(
        group == 0,
        hi,
        jnp.where(
            group == 1,
            mid,
            jnp.where(group == 2, low, jnp.where(group == 3, total_hi, total_low)),
        ),
    )
    return jnp.where(group < 5, packed, 0.0).astype(BF16)


def spread_matrices(width):
    lane = np.arange(LANES)
    columns = np.arange(width + LANES)
    head = np.where(columns < width, columns // (width // HEADS), (columns - width) % HEADS)
    same = (lane[:, None] % HEADS) == head[None, :]
    group = lane[:, None] // HEADS
    peak = same & (group < 3)
    total = same & (group >= 3) & (group < 5)
    return jnp.asarray(peak, BF16), jnp.asarray(total, BF16)


def project_patches(patches, level_ids, sheet_ids, level_ref, w_key, w_value):
    rows, width = patches.shape
    spread = lambda ids: jnp.transpose(
        jnp.broadcast_to(ids.reshape(1, rows).astype(F32), (LANES, rows))
    )
    level = jnp.concatenate([spread(level_ids)] * (width // LANES), axis=1)
    added = jnp.zeros((rows, width), F32)
    for index in range(level_ref.shape[0]):
        added = jnp.where(level == float(index), level_ref[index : index + 1].astype(F32), added)
    key_input = (patches.astype(F32) + added).astype(BF16)
    keys = jnp.dot(key_input, w_key, preferred_element_type=F32).astype(BF16)
    values = jnp.dot(patches, w_value, preferred_element_type=F32).astype(BF16)
    lane = lax.broadcasted_iota(jnp.int32, (rows, LANES), 1)
    return keys, values, (spread(sheet_ids) == lane.astype(F32)).astype(BF16)


def start_all(pairs, sems):
    loads = [
        pltpu.make_async_copy(source, target, sems.at[i]) for i, (source, target) in enumerate(pairs)
    ]
    for load in loads:
        load.start()
    return loads


def cross_kernel(
    level_a_hbm,
    sheet_a_hbm,
    level_b_hbm,
    sheet_b_hbm,
    level_hbm,
    sheets_hbm,
    patch_a_hbm,
    patch_b_hbm,
    queries_hbm,
    pos_hbm,
    proj_hbm,
    out_hbm,
    ids,
    level_ref,
    sheets_ref,
    out_ref,
    patches,
    queries,
    pos,
    proj,
    key_ref,
    value_ref,
    on_ref,
    sems,
    out_sems,
):
    core = lax.axis_index("c")
    groups, rows, width = queries.shape
    half = patch_a_hbm.shape[0]
    block = groups * rows
    head_size = width // HEADS
    loads = start_all(
        (
            (sheets_hbm, sheets_ref),
            (level_hbm, level_ref),
            (level_a_hbm, ids.at[0]),
            (sheet_a_hbm, ids.at[1]),
            (level_b_hbm, ids.at[2]),
            (sheet_b_hbm, ids.at[3]),
            (proj_hbm.at[pl.ds(1, 2)], proj.at[pl.ds(1, 2)]),
            (patch_a_hbm, patches.at[0]),
            (patch_b_hbm, patches.at[1]),
            (proj_hbm.at[0], proj.at[0]),
            (queries_hbm.at[:, core], queries),
            (pos_hbm.at[:, core], pos),
        ),
        sems,
    )
    loads[0].wait()
    sheets = sheets_ref.shape[0]
    barred = jnp.where(sheets_ref[...] == 1, 0.0, NEG)
    barred = jnp.concatenate([barred, jnp.zeros((LANES - sheets, 2 * block), F32)], axis=0)
    barred = jnp.transpose(barred).reshape(groups, 2, rows, LANES)
    barred = jnp.where(core == 0, barred[:, 0], barred[:, 1])
    barred = barred.reshape(block, LANES).astype(BF16)
    for load in loads[1:7]:
        load.wait()
    for i in range(2):
        loads[7 + i].wait()
        cut = pl.ds(i * half, half)
        key_ref[cut], value_ref[cut], on_ref[cut] = project_patches(
            patches[i], ids[2 * i], ids[2 * i + 1], level_ref, proj[1], proj[2]
        )
    for load in loads[9:]:
        load.wait()
    mixed = queries[...].reshape(block, width) + pos[...].reshape(block, width)
    scale = math.log2(math.e) / math.sqrt(head_size)
    q_all = (jnp.dot(mixed, proj[0], preferred_element_type=F32) * scale).astype(BF16)
    lane = lax.broadcasted_iota(jnp.int32, (block, LANES), 1)
    ones = jnp.ones((2 * half, LANES), BF16)
    peaks = jnp.zeros((block, LANES), F32)
    totals = jnp.zeros((block, LANES), F32)
    shape = (groups, rows, LANES)

    def score(head):
        cut = slice(head // 2 * LANES, head // 2 * LANES + LANES)
        inside = lane // head_size == head % 2
        left = jnp.concatenate([jnp.where(inside, q_all[:, cut], 0), barred], axis=1)
        right = jnp.concatenate([key_ref[:, cut], on_ref[...]], axis=1)
        return lax.dot_general(left, right, NT, preferred_element_type=F32)

    def store(cut):
        copy = pltpu.make_async_copy(
            out_ref.at[:, :, cut], out_hbm.at[:, :, cut], out_sems.at[cut.start // LANES]
        )
        copy.start()
        return copy

    scores = score(0)
    stores = []
    sums = None
    for head in range(HEADS):
        now, scores = scores, score(head + 1) if head + 1 < HEADS else None
        cut = slice(head // 2 * LANES, head // 2 * LANES + LANES)
        peak = jnp.max(now, axis=1, keepdims=True)
        weights = jnp.exp2(now - peak).astype(BF16)
        values = jnp.concatenate([value_ref[:, cut], ones], axis=1)
        part = jnp.dot(weights, values, preferred_element_type=F32)
        here = lane % HEADS == head
        peaks = jnp.where(here, peak, peaks)
        totals = jnp.where(here, part[:, LANES:], totals)
        if head % 2 == 0:
            sums = part[:, :LANES]
        else:
            sums = jnp.where(lane // head_size == 0, sums, part[:, :LANES])
            out_ref[:, :, cut] = sums.astype(BF16).reshape(shape)
            stores.append(store(cut))
    out_ref[:, :, width:] = pack_stats(peaks, totals).reshape(shape)
    stores.append(store(slice(width, width + LANES)))
    for copy in stores:
        copy.wait()


def cross_partial(queries, query_pos, query_sheets, own, other, level, proj):
    total, width = queries.shape
    rows = 64
    groups = total // (2 * rows)
    half = own[0].shape[0]
    view = lambda array: array.reshape(groups, 2, rows, array.shape[1])
    hbm = pl.BlockSpec(memory_space=pltpu.HBM)
    return pl.pallas_call(
        cross_kernel,
        in_specs=[hbm] * 11,
        out_specs=hbm,
        scratch_shapes=[
            pltpu.VMEM((4, half), jnp.int32),
            pltpu.VMEM(level.shape, BF16),
            pltpu.VMEM(query_sheets.shape[::-1], jnp.int32),
            pltpu.VMEM((groups, rows, width + LANES), BF16),
            pltpu.VMEM((2, half, width), BF16),
            pltpu.VMEM((groups, rows, width), BF16),
            pltpu.VMEM((groups, rows, width), BF16),
            pltpu.VMEM((3, width, width), BF16),
            pltpu.VMEM((2 * half, width), BF16),
            pltpu.VMEM((2 * half, width), BF16),
            pltpu.VMEM((2 * half, LANES), BF16),
            pltpu.SemaphoreType.DMA((12,)),
            pltpu.SemaphoreType.DMA((width // LANES + 1,)),
        ],
        out_shape=jax.ShapeDtypeStruct((groups, rows, width + LANES), BF16),
        compiler_params=pltpu.CompilerParams(vmem_limit_bytes=LARGE),
        name="cross_partial",
    )(
        *own[1:],
        *other[1:],
        level,
        query_sheets.T,
        own[0],
        other[0],
        view(queries),
        view(query_pos),
        proj,
    )


def combine(parts, peak_matrix, total_matrix):
    width = parts[0].shape[1] - LANES
    stats = [part[:, width:] for part in parts]
    peaks = [jnp.dot(s, peak_matrix, preferred_element_type=F32) for s in stats]
    top = functools.reduce(jnp.maximum, peaks)
    factors = [jnp.exp2(peak - top) for peak in peaks]
    sums = [f[:, :width] * part[:, :width].astype(F32) for f, part in zip(factors, parts)]
    totals = [
        f * jnp.dot(s, total_matrix, preferred_element_type=F32) for f, s in zip(factors, stats)
    ]

    def tree(terms):
        while len(terms) > 1:
            terms = [sum(terms[i : i + 2]) for i in range(0, len(terms), 2)]
        return terms[0]

    return tree(sums), top, tree(totals)


def packed(sums, top, total):
    width = sums.shape[1]
    return jnp.concatenate(
        [sums.astype(BF16), pack_stats(top[:, width:], total[:, width:])], axis=1
    )


def merge_kernel(parts_ref, peak_ref, total_ref, out_ref):
    parts = [parts_ref[i] for i in range(parts_ref.shape[0])]
    out_ref[...] = packed(*combine(parts, peak_ref[...], total_ref[...]))


def merge_two_kernel(a_ref, b_ref, peak_ref, total_ref, out_ref):
    out_ref[...] = packed(*combine([a_ref[...], b_ref[...]], peak_ref[...], total_ref[...]))


def merge(kernel, shape, *operands):
    return pl.pallas_call(
        kernel,
        out_shape=jax.ShapeDtypeStruct(shape, BF16),
        compiler_params=pltpu.CompilerParams(vmem_limit_bytes=SMALL),
        name="merge",
    )(*operands)


def column():
    return lax.axis_index("x") * lax.axis_size("y") + lax.axis_index("y")


def first_kernel(
    a_ref,
    b_ref,
    c_ref,
    d_ref,
    peak_ref,
    total_ref,
    queries_hbm,
    proj_hbm,
    gain_ref,
    out_ref,
    queries,
    weights,
    sems,
):
    loads = start_all(
        ((proj_hbm.at[3], weights), (queries_hbm.at[column(), lax.axis_index("c")], queries)), sems
    )
    parts = [ref[...] for ref in (a_ref, b_ref, c_ref, d_ref)]
    sums, _, total = combine(parts, peak_ref[...], total_ref[...])
    attended = (sums / total[:, : sums.shape[1]]).astype(BF16)
    for load in loads:
        load.wait()
    crossed = jnp.dot(attended, weights[...], preferred_element_type=F32)
    first = layer_norm(queries[...].astype(F32) + crossed, gain_ref[0:1]).astype(BF16)
    for i in range(out_ref.shape[0]):
        out_ref[i] = first


def first_state_of(parts, peak_matrix, total_matrix, queries, proj, gain, copies):
    rows, full = parts[0].shape
    width = full - LANES
    local = pl.BlockSpec(memory_space=pltpu.VMEM)
    hbm = pl.BlockSpec(memory_space=pltpu.HBM)
    return pl.pallas_call(
        first_kernel,
        in_specs=[local] * 6 + [hbm, hbm, local],
        out_specs=local,
        scratch_shapes=[
            pltpu.VMEM((rows, width), BF16),
            pltpu.VMEM((width, width), BF16),
            pltpu.SemaphoreType.DMA((2,)),
        ],
        out_shape=jax.ShapeDtypeStruct((copies, rows, width), BF16),
        compiler_params=pltpu.CompilerParams(vmem_limit_bytes=SMALL),
        name="first_state",
    )(
        *parts,
        peak_matrix,
        total_matrix,
        queries.reshape(copies, 2, rows, width),
        proj,
        gain,
    )


def stack_heads(array, rows):
    stacked = jnp.concatenate([array] * HEADS, axis=0)
    row_head = lax.broadcasted_iota(jnp.int32, stacked.shape, 0) // rows
    col_head = lax.broadcasted_iota(jnp.int32, stacked.shape, 1) // (stacked.shape[1] // HEADS)
    mine = row_head == col_head
    return jnp.where(mine, stacked, 0), mine


def near_kernel(
    first_ref,
    state_ref,
    pos_hbm,
    proj_hbm,
    absorbed_ref,
    mixed_ref,
    stat_ref,
    own_pos,
    pos,
    weights,
    sems,
):
    groups, rows, width = state_ref.shape
    core = lax.axis_index("c")
    loads = start_all(
        (
            (proj_hbm.at[pl.ds(0, 2)], weights),
            (pos_hbm.at[column(), core], own_pos),
            (pos_hbm.at[:, core], pos),
        ),
        sems,
    )
    for load in loads[:2]:
        load.wait()
    scale = math.log2(math.e) / math.sqrt(width // HEADS)
    self_in = first_ref[0] + own_pos[...]
    q_self = jnp.dot(self_in, weights[0], preferred_element_type=F32) * scale
    stacked, _ = stack_heads(q_self.astype(BF16), rows)
    absorbed = lax.dot_general(stacked, weights[1], NT, preferred_element_type=F32).astype(BF16)
    absorbed_ref[...] = absorbed
    state = state_ref[...].reshape(groups * rows, width)
    loads[2].wait()
    inputs = state + pos[...].reshape(groups * rows, width)
    scores = lax.dot_general(absorbed, inputs, NT, preferred_element_type=F32)
    peak = jnp.max(scores, axis=1, keepdims=True)
    weights_here = jnp.exp2(scores - peak)
    total = jnp.sum(weights_here, axis=1, keepdims=True)
    mixed_ref[...] = jnp.dot(weights_here.astype(BF16), state, preferred_element_type=F32)
    lane = lax.broadcasted_iota(jnp.int32, stat_ref.shape, 1)
    stat_ref[...] = jnp.where(lane == 0, peak, total)


def near_half(first, own, query_pos, proj):
    groups, rows, width = own.shape
    local = pl.BlockSpec(memory_space=pltpu.VMEM)
    hbm = pl.BlockSpec(memory_space=pltpu.HBM)
    shapes = [(HEADS * rows, width), (HEADS * rows, width), (HEADS * rows, LANES)]
    return pl.pallas_call(
        near_kernel,
        in_specs=[local, local, hbm, hbm],
        out_specs=[local] * 3,
        scratch_shapes=[
            pltpu.VMEM((rows, width), BF16),
            pltpu.VMEM(own.shape, BF16),
            pltpu.VMEM((2, width, width), BF16),
            pltpu.SemaphoreType.DMA((3,)),
        ],
        out_shape=[
            jax.ShapeDtypeStruct(shape, kind) for shape, kind in zip(shapes, (BF16, F32, F32))
        ],
        compiler_params=pltpu.CompilerParams(vmem_limit_bytes=SMALL),
        cost_estimate=pl.CostEstimate(
            flops=2**33, bytes_accessed=2**22, transcendentals=2**20
        ),
        name="near_half",
    )(first, own, query_pos.reshape(groups, 2, rows, width), proj)


def tail_kernel(
    first_ref,
    absorbed_ref,
    mixed_ref,
    stat_ref,
    state_ref,
    pos_hbm,
    proj_hbm,
    mlp_in_hbm,
    mlp_out_hbm,
    gain_ref,
    out_ref,
    pos,
    proj_ref,
    mlp_in_ref,
    mlp_out_ref,
    sems,
):
    loads = start_all(
        (
            (pos_hbm.at[:, 1 - lax.axis_index("c")], pos),
            (proj_hbm.at[pl.ds(2, 2)], proj_ref),
            (mlp_in_hbm, mlp_in_ref),
            (mlp_out_hbm, mlp_out_ref),
        ),
        sems,
    )
    _, rows, width = first_ref.shape
    keys = state_ref.shape[0] * state_ref.shape[1]
    state = state_ref[...].reshape(keys, width)
    loads[0].wait()
    inputs = state + pos[...].reshape(keys, width)
    scores = lax.dot_general(absorbed_ref[...], inputs, NT, preferred_element_type=F32)
    peak_a, total_a = stat_ref[:, 0:1], stat_ref[:, 1:2]
    peak_b = jnp.max(scores, axis=1, keepdims=True)
    peak = jnp.maximum(peak_a, peak_b)
    weights = jnp.exp2(scores - peak)
    factor = jnp.exp2(peak_a - peak)
    total = factor * total_a + jnp.sum(weights, axis=1, keepdims=True)
    mixed = factor * mixed_ref[...]
    mixed += jnp.dot(weights.astype(BF16), state, preferred_element_type=F32)
    mixed = (mixed / total).astype(BF16)
    loads[1].wait()
    blended = jnp.dot(mixed, proj_ref[0], preferred_element_type=F32)
    head_size = width // HEADS
    column = lax.broadcasted_iota(jnp.int32, (rows, width), 1) // head_size
    self_out = jnp.zeros((rows, width), F32)
    for head in range(HEADS):
        self_out = jnp.where(column == head, blended[head * rows : (head + 1) * rows], self_out)
    second = first_ref[0].astype(F32) + jnp.dot(
        self_out.astype(BF16), proj_ref[1], preferred_element_type=F32
    )
    second = layer_norm(second, gain_ref[1:2]).astype(BF16)
    loads[2].wait()
    hidden = jnp.dot(second, mlp_in_ref[...], preferred_element_type=F32)
    hidden = jnp.maximum(hidden, 0.0).astype(BF16)
    loads[3].wait()
    decoded = second.astype(F32) + jnp.dot(hidden, mlp_out_ref[...], preferred_element_type=F32)
    out_ref[...] = layer_norm(decoded, gain_ref[2:3]).astype(BF16)


def tail(first, partial, other, query_pos, proj, mlp_in, mlp_out, gain):
    groups, rows, width = other.shape
    local = pl.BlockSpec(memory_space=pltpu.VMEM)
    hbm = pl.BlockSpec(memory_space=pltpu.HBM)
    return pl.pallas_call(
        tail_kernel,
        in_specs=[local] * 5 + [hbm] * 4 + [local],
        out_specs=local,
        scratch_shapes=[
            pltpu.VMEM(other.shape, BF16),
            pltpu.VMEM((2, width, width), BF16),
            pltpu.VMEM(mlp_in.shape, BF16),
            pltpu.VMEM(mlp_out.shape, BF16),
            pltpu.SemaphoreType.DMA((4,)),
        ],
        out_shape=jax.ShapeDtypeStruct((rows, width), BF16),
        compiler_params=pltpu.CompilerParams(vmem_limit_bytes=SMALL),
        name="tail",
    )(
        first,
        *partial,
        other,
        query_pos.reshape(groups, 2, rows, width),
        proj,
        mlp_in,
        mlp_out,
        gain,
    )


def body(
    queries,
    query_pos,
    patches,
    patch_level,
    patch_sheet,
    query_sheets,
    level_embed,
    cross_proj,
    self_proj,
    mlp_in,
    mlp_out,
    norm_gain,
):
    square = lax.axis_size("x") * lax.axis_size("y")
    bands = lax.axis_size("z")
    swap = [(0, 1), (1, 0)]
    own = (patches, patch_level, patch_sheet)
    other = [lax.ppermute(array, "c", swap) for array in own]
    spread = spread_matrices(queries.shape[1])
    parts = cross_partial(queries, query_pos, query_sheets, own, other, level_embed, cross_proj)
    parts = lax.all_to_all(parts, ("x", "y"), 0, 0, tiled=True)
    part = merge(merge_kernel, parts.shape[1:], parts, *spread)
    part = merge(
        merge_two_kernel,
        part.shape,
        part,
        lax.ppermute(part, "z", [(i, i ^ 1) for i in range(bands)]),
        *spread,
    )
    sign = lambda i: 1 - 2 * (i % 2)
    shift = lambda hop: lax.ppermute(
        part, "z", [(i, (i + hop * sign(i)) % bands) for i in range(bands)]
    )
    near, middle, far = shift(-1), shift(-2), shift(-3)
    first = first_state_of(
        (part, far, near, middle),
        *spread,
        queries,
        cross_proj,
        norm_gain,
        square,
    )
    own = lax.all_to_all(first, ("x", "y"), 0, 0, tiled=True)
    other = lax.ppermute(own, "c", swap)
    partial = near_half(first, own, query_pos, self_proj)
    return tail(first, partial, other, query_pos, self_proj, mlp_in, mlp_out, norm_gain)


def solution(mesh):
    devices = mesh.devices
    names = ("z", "x", "y", "c")
    grid = Mesh(devices.reshape(devices.shape[0], 4, 4, 2), names)
    return jax.shard_map(
        body,
        mesh=grid,
        in_specs=(P(), P(), P(names, None), P(names), P(names)) + (P(),) * 7,
        out_specs=P(names[1:], None),
        check_vma=False,
    )
```

time: 615 us -> 93.3 us (0.15)
  waiting for transfers between devices: 313 us -> 7.44 us
  local copies, waits for them, and re-layouts: 95.3 us -> 0.83 us
  matrix products: 72.7 us -> 0 us
  blocking collectives: 95.5 us -> 41.1 us
  Pallas kernels: 0 us -> 24.8 us
  other arithmetic: 22.9 us -> 0 us
  starting transfers between devices: 0.17 us -> 18.6 us
  between operations: 13.3 us -> 0.29 us
    all_gather x2 -> x0, waiting for transfers between devices: 91.7 us -> none  [the longest x1 49.5 us: body(): lax.all_gather(k_self, 'tile', axis=0, tiled=True)]
    unnamed x6 -> x0, waiting for transfers between devices: 87.7 us -> none
    pmax x1 -> x0, blocking collectives: 81.6 us -> none  [body(): lax.pmax(local_peak.astype(jnp.bfloat16), ('band', 'tile'))]
    reduce_scatter x1 -> x0, waiting for transfers between devices: 79.2 us -> none  [body(): lax.psum_scatter(numer.astype(jnp.bfloat16), 'tile', scatter_dimension=0,...]
    dot_general x22 -> x0, matrix products: 68 us -> none  [the longest x4 23.2 us: block_masked(): jnp.einsum('qhe,phe->hqp', q_part, k_heads, preferred_element_type=jnp.fl...]
    dynamic_slice x8 -> x0, local copies, waits for them, and re-layouts: 67.4 us -> none  [body(): numer, denom = lax.map(block_sums, (masked_all, peak))]
    psum x1 -> x0, waiting for transfers between devices: 54.8 us -> none  [body(): lax.psum(numer_tile.astype(jnp.bfloat16), 'band').astype(jnp.float32)]
    all_to_all x0 -> x2, blocking collectives: none -> 41.1 us  [the longest x1 24.2 us: body(): parts = lax.all_to_all(parts, ('x', 'y'), 0, 0, tiled=True)]
  transfers between devices with their start and end apart: 5 -> 8, of which waited for: 5 -> 4; matrix products, arithmetic and copies ran while one was open for 2% -> 0% of each run, Pallas kernels for 0% -> 3%
where the time goes in v2:
time: 93.3 us; the launch traced here: 93.1 us
  blocking collectives  41.1 us (44%)
  Pallas kernels  24.8 us (27%)
  starting transfers between devices  18.6 us (20%)
  waiting for transfers between devices  7.44 us (8%)
    all_to_all x1, blocking collectives, body(): parts = lax.all_to_all(parts, ('x', 'y'), 0, 0, tiled=True)  24.2 us
    all_to_all x1, blocking collectives, body(): own = lax.all_to_all(first, ('x', 'y'), 0, 0, tiled=True)  16.9 us
    pallas_call x1, Pallas kernels, cross_partial(): pl.pallas_call(cross_kernel, in_specs=[hbm] * 11, out_specs=hbm, scratch_...  14.9 us
    ppermute x3, starting transfers between devices, body(): lax.ppermute(part, 'z', [(i, (i + hop * sign(i)) % bands) for i in range(...  8.28 us
    pallas_call x1, Pallas kernels, tail(): pl.pallas_call(tail_kernel, in_specs=[local] * 5 + [hbm] * 4 + [local], o...  5.27 us
    ppermute x1, starting transfers between devices, body(): other = lax.ppermute(own, 'c', swap)  4.88 us
    ppermute x3, waiting for transfers between devices, body(): lax.ppermute(part, 'z', [(i, (i + hop * sign(i)) % bands) for i in range(...  4.36 us
    ppermute x3, starting transfers between devices, body(): other = [lax.ppermute(array, 'c', swap) for array in own]  3.75 us
  transfers between devices with their start and end apart: 8, of which 4 were waited for; matrix products, arithmetic and copies ran while one was open for 0% of the time, Pallas kernels for 3%

profile of v2, /device:TPU:1, one launch (start us, length us, event | category | flops | bytes accessed | tf_op | source)
XLA Modules:
  0.0 93.1 jit_solution(14133354362894174317)
XLA Ops:
  0.0 3.2 %collective-permute-start.2 = (bf16[512,512]{1,0:T(8,128)(2,1)}, bf16[512,512]{1,0:T(8,128)(2,1)S(1)}, u32[]{:S(2)}, u32[]{:S(2)}) collective-permute-start(bf16[512,512]{1,0:T(8,128)(2,1)} %patch_a_hbm.1), channel_id=1, source_target_pairs={{0,1},{1,0},{2,3},{3,2},{4,5},{5,4},{6,7},{7,6},{8,9},{9,8},{10,11... | collective-permute-start | bytes 1572872 | tf_op jit(solution)/shard_map/ppermute | solution.py:532
  3.2 0.0 collective-permute-start
  3.2 0.5 collective-permute-start.1
  3.8 1.2 %collective-permute-done.level_b_hbm = s32[512]{0:T(512)S(1)} collective-permute-done((s32[512]{0:T(512)}, s32[512]{0:T(512)S(1)}, u32[]{:S(2)}, u32[]{:S(2)}) %collective-permute-start) | collective-permute-done | bytes 2080 | tf_op jit(solution)/shard_map/ppermute | solution.py:532
  5.0 0.0 copy-start.10
  5.0 0.0 collective-permute-done.1.sheet_b_hbm
  5.0 0.0 copy-start.11
  5.0 0.0 collective-permute-done.2.patch_b_hbm
  5.0 0.0 copy-start.9
  5.0 0.6 copy-done.10
  5.6 0.0 copy-done.11
  5.6 0.2 copy-done.9
  5.8 0.0 copy-start.6
  5.8 0.0 copy-start.7
  5.8 14.9 %cross_partial.1 = bf16[16,64,640]{2,1,0:T(8,128)(2,1)} custom-call(s32[512]{0:T(512)} %level_a_hbm.1, s32[512]{0:T(512)} %sheet_a_hbm.1, s32[512]{0:T(512)} %copy-done.10, s32[512]{0:T(512)} %copy-done.11, bf16[4,512]{1,0:T(4,128)(2,1)} %level_hbm.1, s32[16,2048]{1,0:T(8,128)} %bitcast.8, bf16[512,512]{1,0:T(8,128)(2,1)} %patch_a_hbm.1, ...), custom_call_target="tpu_custom_call" | custom-call | tf_op jit(solution)/shard_map/cross_partial/pallas_call | solution.py:207
  20.7 0.0 copy-start
  20.7 0.0 copy-start.1
  20.7 0.0 copy-start.8
  20.7 24.2 %all_to_all.10.parts_ref = bf16[16,64,640]{2,1,0:T(8,128)(2,1)S(1)} all-to-all(bf16[16,64,640]{2,1,0:T(8,128)(2,1)} %cross_partial.1), channel_id=1, replica_groups=mesh['z'=8,'x'=4,'y'=4,'c'=2] {'x','y'}, dimensions={0} | all-to-all | bytes 2621440 | tf_op jit(solution)/shard_map/all_to_all | solution.py:535
  44.9 0.0 copy-done.6
  44.9 0.0 copy-done.7
  44.9 1.0 %merge.2.a_ref = bf16[64,640]{1,0:T(8,128)(2,1)S(1)} custom-call(bf16[16,64,640]{2,1,0:T(8,128)(2,1)S(1)} %all_to_all.10.parts_ref, bf16[128,640]{1,0:T(8,128)(2,1)S(1)} %copy-done.7, bf16[128,640]{1,0:T(8,128)(2,1)S(1)} %copy-done.6), custom_call_target="tpu_custom_call" | custom-call | tf_op jit(solution)/shard_map/merge/pallas_call | solution.py:278
  45.9 1.7 %collective-permute-start.3 = (bf16[64,640]{1,0:T(8,128)(2,1)S(1)}, bf16[64,640]{1,0:T(8,128)(2,1)S(1)}, u32[]{:S(2)}, u32[]{:S(2)}) collective-permute-start(bf16[64,640]{1,0:T(8,128)(2,1)S(1)} %merge.2.a_ref), channel_id=1, source_target_pairs={{0,32},{32,0},{64,96},{96,64},{128,160},{160,128},{192,224},{224,1... | collective-permute-start | bytes 245768 | tf_op jit(solution)/shard_map/ppermute | solution.py:541
  47.7 1.8 %collective-permute-done.3.b_ref = bf16[64,640]{1,0:T(8,128)(2,1)S(1)} collective-permute-done((bf16[64,640]{1,0:T(8,128)(2,1)S(1)}, bf16[64,640]{1,0:T(8,128)(2,1)S(1)}, u32[]{:S(2)}, u32[]{:S(2)}) %collective-permute-start.3) | collective-permute-done | bytes 81952 | tf_op jit(solution)/shard_map/ppermute | solution.py:541
  49.5 0.2 merge.3.a_ref
  49.7 5.9 %collective-permute-start.6 = (bf16[64,640]{1,0:T(8,128)(2,1)S(1)}, bf16[64,640]{1,0:T(8,128)(2,1)S(1)}, u32[]{:S(2)}, u32[]{:S(2)}) collective-permute-start(bf16[64,640]{1,0:T(8,128)(2,1)S(1)} %merge.3.a_ref), channel_id=1, source_target_pairs={{0,192},{32,96},{64,0},{96,160},{128,64},{160,224},{192,128},{224,... | collective-permute-start | bytes 245768 | tf_op jit(solution)/shard_map/ppermute | solution.py:545
  55.7 0.0 collective-permute-start.5
  55.7 2.3 %collective-permute-start.4 = (bf16[64,640]{1,0:T(8,128)(2,1)S(1)}, bf16[64,640]{1,0:T(8,128)(2,1)S(1)}, u32[]{:S(2)}, u32[]{:S(2)}) collective-permute-start(bf16[64,640]{1,0:T(8,128)(2,1)S(1)} %merge.3.a_ref), channel_id=1, source_target_pairs={{0,160},{32,128},{64,224},{96,192},{128,32},{160,0},{192,96},{224,... | collective-permute-start | bytes 245768 | tf_op jit(solution)/shard_map/ppermute | solution.py:545
  58.0 0.0 collective-permute-done.6.d_ref
  58.0 3.0 %collective-permute-done.5.c_ref = bf16[64,640]{1,0:T(8,128)(2,1)S(1)} collective-permute-done((bf16[64,640]{1,0:T(8,128)(2,1)S(1)}, bf16[64,640]{1,0:T(8,128)(2,1)S(1)}, u32[]{:S(2)}, u32[]{:S(2)}) %collective-permute-start.5) | collective-permute-done | bytes 81952 | tf_op jit(solution)/shard_map/ppermute | solution.py:545
  61.0 1.3 %collective-permute-done.4.b_ref = bf16[64,640]{1,0:T(8,128)(2,1)S(1)} collective-permute-done((bf16[64,640]{1,0:T(8,128)(2,1)S(1)}, bf16[64,640]{1,0:T(8,128)(2,1)S(1)}, u32[]{:S(2)}, u32[]{:S(2)}) %collective-permute-start.4) | collective-permute-done | bytes 81952 | tf_op jit(solution)/shard_map/ppermute | solution.py:545
  62.4 0.0 copy-done
  62.4 0.0 copy-done.1
  62.4 0.0 copy-done.8
  62.4 0.0 copy-start.3
  62.4 1.0 %first_state.1.first_ref = bf16[16,64,512]{2,1,0:T(8,128)(2,1)S(1)} custom-call(bf16[64,640]{1,0:T(8,128)(2,1)S(1)} %merge.3.a_ref, bf16[64,640]{1,0:T(8,128)(2,1)S(1)} %collective-permute-done.4.b_ref, bf16[64,640]{1,0:T(8,128)(2,1)S(1)} %collective-permute-done.5.c_ref, bf16[64,640]{1,0:T(8,128)(2,1)S(1)} %collective-permute-done.6.d_ref, ...), custom_call_target="tpu_custom_call" | custom-call | tf_op jit(solution)/shard_map/first_state/pallas_call | solution.py:324
  63.4 0.0 copy-start.2
  63.4 16.9 %all_to_all.11.state_ref = bf16[16,64,512]{2,1,0:T(8,128)(2,1)S(1)} all-to-all(bf16[16,64,512]{2,1,0:T(8,128)(2,1)S(1)} %first_state.1.first_ref), channel_id=1, replica_groups=mesh['z'=8,'x'=4,'y'=4,'c'=2] {'x','y'}, dimensions={0} | all-to-all | bytes 2097152 | tf_op jit(solution)/shard_map/all_to_all | solution.py:557
  80.3 0.0 copy-start.4
  80.3 0.0 copy-start.5
  80.3 4.9 %collective-permute-start.7 = (bf16[16,64,512]{2,1,0:T(8,128)(2,1)S(1)}, bf16[16,64,512]{2,1,0:T(8,128)(2,1)S(1)}, u32[]{:S(2)}, u32[]{:S(2)}) collective-permute-start(bf16[16,64,512]{2,1,0:T(8,128)(2,1)S(1)} %all_to_all.11.state_ref), channel_id=1, source_target_pairs={{0,1},{1,0},{2,3},{3,2},{4,5},{5,4},{6,7},{7,6},{8,9},{9,8},{10,11... | collective-permute-start | bytes 3145736 | tf_op jit(solution)/shard_map/ppermute | solution.py:558
  85.2 0.0 copy-done.3
  85.2 0.0 copy-done.2
  85.2 2.5 %near_half.1 = (bf16[512,512]{1,0:T(8,128)(2,1)S(1)}, f32[512,512]{1,0:T(8,128)S(1)}, f32[512,128]{1,0:T(8,128)S(1)}) custom-call(bf16[16,64,512]{2,1,0:T(8,128)(2,1)S(1)} %first_state.1.first_ref, bf16[16,64,512]{2,1,0:T(8,128)(2,1)S(1)} %all_to_all.11.state_ref, bf16[16,2,64,512]{3,2,1,0:T(8,128)(2,1)S(1)} %bitcast.6, bf16[4,512,512]{2,1,0:T(8,128)(2,1)S(1)} %copy-done.3), custom_call_target="tpu_custom_call" | custom-call | flops 8589934592 | bytes 4194304 | tf_op jit(solution)/shard_map/near_half/pallas_call | solution.py:402
  87.7 0.0 collective-permute-done.7.state_ref
  87.7 0.0 copy-done.4
  87.7 0.0 copy-done.5
  87.7 5.3 %tail.1 = bf16[64,512]{1,0:T(8,128)(2,1)} custom-call(bf16[16,64,512]{2,1,0:T(8,128)(2,1)S(1)} %first_state.1.first_ref, bf16[512,512]{1,0:T(8,128)(2,1)S(1)} %get-tuple-element.8.absorbed_ref, f32[512,512]{1,0:T(8,128)S(1)} %get-tuple-element.9.mixed_ref, f32[512,128]{1,0:T(8,128)S(1)} %get-tuple-element.10.stat_ref, ...), custom_call_target="tpu_custom_call" | custom-call | tf_op jit(solution)/shard_map/tail/pallas_call | solution.py:488
Async XLA Ops:
  0.0 5.0 %collective-permute-start.2 = (bf16[512,512]{1,0:T(8,128)(2,1)}, bf16[512,512]{1,0:T(8,128)(2,1)S(1)}, u32[]{:S(2)}, u32[]{:S(2)}) collective-permute-start(bf16[512,512]{1,0:T(8,128)(2,1)} %patch_a_hbm.1), channel_id=1, source_target_pairs={{0,1},{1,0},{2,3},{3,2},{4,5},{5,4},{6,7},{7,6},{8,9},{9,8},{10,11... | collective-permute-start | bytes 1572872 | tf_op jit(solution)/shard_map/ppermute | solution.py:532
  3.2 1.8 %collective-permute-start = (s32[512]{0:T(512)}, s32[512]{0:T(512)S(1)}, u32[]{:S(2)}, u32[]{:S(2)}) collective-permute-start(s32[512]{0:T(512)} %level_a_hbm.1), channel_id=1, source_target_pairs={{0,1},{1,0},{2,3},{3,2},{4,5},{5,4},{6,7},{7,6},{8,9},{9,8},{10,11... | collective-permute-start | bytes 6152 | tf_op jit(solution)/shard_map/ppermute | solution.py:532
  3.2 1.8 %collective-permute-start.1 = (s32[512]{0:T(512)}, s32[512]{0:T(512)S(1)}, u32[]{:S(2)}, u32[]{:S(2)}) collective-permute-start(s32[512]{0:T(512)} %sheet_a_hbm.1), channel_id=1, source_target_pairs={{0,1},{1,0},{2,3},{3,2},{4,5},{5,4},{6,7},{7,6},{8,9},{9,8},{10,11... | collective-permute-start | bytes 6152 | tf_op jit(solution)/shard_map/ppermute | solution.py:532
  5.0 0.6 copy-start.10
  5.0 0.6 copy-start.11
  5.0 0.8 copy-start.9
  5.8 39.1 %copy-start.6 = (bf16[128,640]{1,0:T(8,128)(2,1)S(1)}, bf16[128,640]{1,0:T(8,128)(2,1)}, u32[]{:S(2)}) copy-start(bf16[128,640]{1,0:T(8,128)(2,1)} %constant.5.clone.total_ref) | copy-start | bytes 491524
  5.8 39.1 %copy-start.7 = (bf16[128,640]{1,0:T(8,128)(2,1)S(1)}, bf16[128,640]{1,0:T(8,128)(2,1)}, u32[]{:S(2)}) copy-start(bf16[128,640]{1,0:T(8,128)(2,1)} %constant.4.clone.peak_ref) | copy-start | bytes 491524
  20.7 41.7 %copy-start = (bf16[2048,512]{1,0:T(8,128)(2,1)S(1)}, bf16[2048,512]{1,0:T(8,128)(2,1)}, u32[]{:S(2)}) copy-start(bf16[2048,512]{1,0:T(8,128)(2,1)} %param.14) | copy-start | bytes 6291460
  20.7 41.7 %copy-start.1 = (bf16[4,512,512]{2,1,0:T(8,128)(2,1)S(1)}, bf16[4,512,512]{2,1,0:T(8,128)(2,1)}, u32[]{:S(2)}) copy-start(bf16[4,512,512]{2,1,0:T(8,128)(2,1)} %proj_hbm.5) | copy-start | bytes 6291460
  20.7 41.7 %copy-start.8 = (f32[3,512]{1,0:T(4,128)S(1)}, f32[3,512]{1,0:T(4,128)}, u32[]{:S(2)}) copy-start(f32[3,512]{1,0:T(4,128)} %gain_ref.3) | copy-start | bytes 18436
  45.9 3.6 %collective-permute-start.3 = (bf16[64,640]{1,0:T(8,128)(2,1)S(1)}, bf16[64,640]{1,0:T(8,128)(2,1)S(1)}, u32[]{:S(2)}, u32[]{:S(2)}) collective-permute-start(bf16[64,640]{1,0:T(8,128)(2,1)S(1)} %merge.2.a_ref), channel_id=1, source_target_pairs={{0,32},{32,0},{64,96},{96,64},{128,160},{160,128},{192,224},{224,1... | collective-permute-start | bytes 245768 | tf_op jit(solution)/shard_map/ppermute | solution.py:541
  49.7 8.3 %collective-permute-start.6 = (bf16[64,640]{1,0:T(8,128)(2,1)S(1)}, bf16[64,640]{1,0:T(8,128)(2,1)S(1)}, u32[]{:S(2)}, u32[]{:S(2)}) collective-permute-start(bf16[64,640]{1,0:T(8,128)(2,1)S(1)} %merge.3.a_ref), channel_id=1, source_target_pairs={{0,192},{32,96},{64,0},{96,160},{128,64},{160,224},{192,128},{224,... | collective-permute-start | bytes 245768 | tf_op jit(solution)/shard_map/ppermute | solution.py:545
  55.7 5.4 %collective-permute-start.5 = (bf16[64,640]{1,0:T(8,128)(2,1)S(1)}, bf16[64,640]{1,0:T(8,128)(2,1)S(1)}, u32[]{:S(2)}, u32[]{:S(2)}) collective-permute-start(bf16[64,640]{1,0:T(8,128)(2,1)S(1)} %merge.3.a_ref), channel_id=1, source_target_pairs={{0,224},{32,64},{64,32},{96,128},{128,96},{160,192},{192,160},{224... | collective-permute-start | bytes 245768 | tf_op jit(solution)/shard_map/ppermute | solution.py:545
  55.7 6.7 %collective-permute-start.4 = (bf16[64,640]{1,0:T(8,128)(2,1)S(1)}, bf16[64,640]{1,0:T(8,128)(2,1)S(1)}, u32[]{:S(2)}, u32[]{:S(2)}) collective-permute-start(bf16[64,640]{1,0:T(8,128)(2,1)S(1)} %merge.3.a_ref), channel_id=1, source_target_pairs={{0,160},{32,128},{64,224},{96,192},{128,32},{160,0},{192,96},{224,... | collective-permute-start | bytes 245768 | tf_op jit(solution)/shard_map/ppermute | solution.py:545
  62.4 22.8 %copy-start.3 = (bf16[4,512,512]{2,1,0:T(8,128)(2,1)S(1)}, bf16[4,512,512]{2,1,0:T(8,128)(2,1)}, u32[]{:S(2)}) copy-start(bf16[4,512,512]{2,1,0:T(8,128)(2,1)} %proj_hbm.7) | copy-start | bytes 6291460
  63.4 21.8 %copy-start.2 = (bf16[2048,512]{1,0:T(8,128)(2,1)S(1)}, bf16[2048,512]{1,0:T(8,128)(2,1)}, u32[]{:S(2)}) copy-start(bf16[2048,512]{1,0:T(8,128)(2,1)} %param.15) | copy-start | bytes 6291460
  80.3 7.4 %copy-start.4 = (bf16[512,2048]{1,0:T(8,128)(2,1)S(1)}, bf16[512,2048]{1,0:T(8,128)(2,1)}, u32[]{:S(2)}) copy-start(bf16[512,2048]{1,0:T(8,128)(2,1)} %mlp_in_hbm.1) | copy-start | bytes 6291460
  80.3 7.4 %copy-start.5 = (bf16[2048,512]{1,0:T(8,128)(2,1)S(1)}, bf16[2048,512]{1,0:T(8,128)(2,1)}, u32[]{:S(2)}) copy-start(bf16[2048,512]{1,0:T(8,128)(2,1)} %mlp_out_hbm.1) | copy-start | bytes 6291460
  80.3 7.4 %collective-permute-start.7 = (bf16[16,64,512]{2,1,0:T(8,128)(2,1)S(1)}, bf16[16,64,512]{2,1,0:T(8,128)(2,1)S(1)}, u32[]{:S(2)}, u32[]{:S(2)}) collective-permute-start(bf16[16,64,512]{2,1,0:T(8,128)(2,1)S(1)} %all_to_all.11.state_ref), channel_id=1, source_target_pairs={{0,1},{1,0},{2,3},{3,2},{4,5},{5,4},{6,7},{7,6},{8,9},{9,8},{10,11... | collective-permute-start | bytes 3145736 | tf_op jit(solution)/shard_map/ppermute | solution.py:558

commit v3 on v2

--- a/solution.py
+++ b/solution.py
@@ -3,7 +3,6 @@
 
 import jax
 import jax.numpy as jnp
-import numpy as np
 from jax import lax
 from jax.experimental import pallas as pl
 from jax.experimental.pallas import tpu as pltpu
@@ -14,7 +13,7 @@
 LANES = 128
 NEG = -1e30
 SMALL = 32 * 2**20
-LARGE = 60 * 2**20
+LARGE = 63_400_000
 NT = (((1,), (1,)), ((), ()))
 F32 = jnp.float32
 BF16 = jnp.bfloat16
@@ -27,51 +26,22 @@
     return shifted * lax.rsqrt(spread + 1e-05) * gain
 
 
-def pack_stats(peak, total):
-    hi = peak.astype(BF16).astype(F32)
-    rest = peak - hi
-    mid = rest.astype(BF16).astype(F32)
-    low = rest - mid
-    total_hi = total.astype(BF16).astype(F32)
-    total_low = total - total_hi
-    group = lax.broadcasted_iota(jnp.int32, peak.shape, 1) // HEADS
-    packed = jnp.where(
-        group == 0,
-        hi,
-        jnp.where(
-            group == 1,
-            mid,
-            jnp.where(group == 2, low, jnp.where(group == 3, total_hi, total_low)),
-        ),
-    )
-    return jnp.where(group < 5, packed, 0.0).astype(BF16)
-
-
-def spread_matrices(width):
-    lane = np.arange(LANES)
-    columns = np.arange(width + LANES)
-    head = np.where(columns < width, columns // (width // HEADS), (columns - width) % HEADS)
-    same = (lane[:, None] % HEADS) == head[None, :]
-    group = lane[:, None] // HEADS
-    peak = same & (group < 3)
-    total = same & (group >= 3) & (group < 5)
-    return jnp.asarray(peak, BF16), jnp.asarray(total, BF16)
-
-
-def project_patches(patches, level_ids, sheet_ids, level_ref, w_key, w_value):
+def pieces(value):
+    hi = value.astype(BF16).astype(F32)
+    mid = (value - hi).astype(BF16).astype(F32)
+    return hi, mid, value - hi - mid
+
+
+def project_patches(patches, level_ids, sheet_ids, sheets, level_rows, w_key, w_value):
     rows, width = patches.shape
-    spread = lambda ids: jnp.transpose(
-        jnp.broadcast_to(ids.reshape(1, rows).astype(F32), (LANES, rows))
-    )
-    level = jnp.concatenate([spread(level_ids)] * (width // LANES), axis=1)
-    added = jnp.zeros((rows, width), F32)
-    for index in range(level_ref.shape[0]):
-        added = jnp.where(level == float(index), level_ref[index : index + 1].astype(F32), added)
+    row = lax.broadcasted_iota(jnp.int32, (LANES, rows), 0)
+    held = (row == sheet_ids.reshape(1, rows)) | (row == level_ids.reshape(1, rows) + sheets)
+    held = jnp.transpose(jnp.where(held, 1.0, 0.0)).astype(BF16)
+    added = jnp.dot(held, level_rows, preferred_element_type=F32)
     key_input = (patches.astype(F32) + added).astype(BF16)
     keys = jnp.dot(key_input, w_key, preferred_element_type=F32).astype(BF16)
     values = jnp.dot(patches, w_value, preferred_element_type=F32).astype(BF16)
-    lane = lax.broadcasted_iota(jnp.int32, (rows, LANES), 1)
-    return keys, values, (spread(sheet_ids) == lane.astype(F32)).astype(BF16)
+    return keys, values, held
 
 
 def start_all(pairs, sems):
@@ -134,18 +104,30 @@
     )
     loads[0].wait()
     sheets = sheets_ref.shape[0]
-    barred = jnp.where(sheets_ref[...] == 1, 0.0, NEG)
-    barred = jnp.concatenate([barred, jnp.zeros((LANES - sheets, 2 * block), F32)], axis=0)
-    barred = jnp.transpose(barred).reshape(groups, 2, rows, LANES)
-    barred = jnp.where(core == 0, barred[:, 0], barred[:, 1])
-    barred = barred.reshape(block, LANES).astype(BF16)
+    cut = lax.broadcasted_iota(jnp.int32, (sheets, LANES), 1) < rows
+    picked = []
+    for start in range(0, 2 * block, 2 * LANES):
+        even = sheets_ref[:, start : start + LANES]
+        odd = sheets_ref[:, start + LANES : start + 2 * LANES]
+        low = jnp.where(cut, even, pltpu.roll(odd, rows, 1))
+        high = jnp.where(cut, pltpu.roll(even, rows, 1), odd)
+        picked.append(jnp.where(core == 0, low, high))
+    barred = jnp.where(jnp.concatenate(picked, axis=1) == 1, 0.0, NEG)
+    barred = jnp.concatenate([barred, jnp.zeros((LANES - sheets, block), F32)], axis=0)
+    barred = jnp.transpose(barred).astype(BF16)
     for load in loads[1:7]:
         load.wait()
+    row = lax.broadcasted_iota(jnp.int32, (LANES, width), 0)
+    level_rows = jnp.zeros((LANES, width), F32)
+    for index in range(level_ref.shape[0]):
+        added = level_ref[index : index + 1].astype(F32)
+        level_rows = jnp.where(row == sheets + index, added, level_rows)
+    level_rows = level_rows.astype(BF16)
     for i in range(2):
         loads[7 + i].wait()
         cut = pl.ds(i * half, half)
         key_ref[cut], value_ref[cut], on_ref[cut] = project_patches(
-            patches[i], ids[2 * i], ids[2 * i + 1], level_ref, proj[1], proj[2]
+            patches[i], ids[2 * i], ids[2 * i + 1], sheets, level_rows, proj[1], proj[2]
         )
     for load in loads[9:]:
         load.wait()
@@ -156,7 +138,6 @@
     ones = jnp.ones((2 * half, LANES), BF16)
     peaks = jnp.zeros((block, LANES), F32)
     totals = jnp.zeros((block, LANES), F32)
-    shape = (groups, rows, LANES)
 
     def score(head):
         cut = slice(head // 2 * LANES, head // 2 * LANES + LANES)
@@ -173,7 +154,6 @@
         return copy
 
     scores = score(0)
-    stores = []
     sums = None
     for head in range(HEADS):
         now, scores = scores, score(head + 1) if head + 1 < HEADS else None
@@ -189,10 +169,20 @@
             sums = part[:, :LANES]
         else:
             sums = jnp.where(lane // head_size == 0, sums, part[:, :LANES])
-            out_ref[:, :, cut] = sums.astype(BF16).reshape(shape)
-            stores.append(store(cut))
-    out_ref[:, :, width:] = pack_stats(peaks, totals).reshape(shape)
-    stores.append(store(slice(width, width + LANES)))
+            sums = sums.astype(BF16).reshape(groups, rows, LANES)
+            for group in range(groups):
+                out_ref[group, :rows, cut] = sums[group]
+    kind = lane // HEADS
+    hi, mid, low = pieces(peaks)
+    stats = jnp.where(kind == 0, hi, jnp.where(kind == 1, mid, jnp.where(kind == 2, low, totals)))
+    stats = jnp.transpose(stats)
+    for group in range(0, groups, 2):
+        cut = slice(group * rows, group * rows + LANES)
+        tile = [stats[k * HEADS : k * HEADS + HEADS, cut] for k in range(width // LANES)]
+        tile = jnp.concatenate(tile, axis=1).astype(BF16)
+        out_ref[group, rows:] = tile
+        out_ref[group + 1, rows:] = tile
+    stores = [store(slice(i, i + LANES)) for i in range(0, width, LANES)]
     for copy in stores:
         copy.wait()
 
@@ -212,7 +202,7 @@
             pltpu.VMEM((4, half), jnp.int32),
             pltpu.VMEM(level.shape, BF16),
             pltpu.VMEM(query_sheets.shape[::-1], jnp.int32),
-            pltpu.VMEM((groups, rows, width + LANES), BF16),
+            pltpu.VMEM((groups, rows + HEADS, width), BF16),
             pltpu.VMEM((2, half, width), BF16),
             pltpu.VMEM((groups, rows, width), BF16),
             pltpu.VMEM((groups, rows, width), BF16),
@@ -221,9 +211,9 @@
             pltpu.VMEM((2 * half, width), BF16),
             pltpu.VMEM((2 * half, LANES), BF16),
             pltpu.SemaphoreType.DMA((12,)),
-            pltpu.SemaphoreType.DMA((width // LANES + 1,)),
+            pltpu.SemaphoreType.DMA((width // LANES,)),
         ],
-        out_shape=jax.ShapeDtypeStruct((groups, rows, width + LANES), BF16),
+        out_shape=jax.ShapeDtypeStruct((groups, rows + HEADS, width), BF16),
         compiler_params=pltpu.CompilerParams(vmem_limit_bytes=LARGE),
         name="cross_partial",
     )(
@@ -239,39 +229,58 @@
     )
 
 
-def combine(parts, peak_matrix, total_matrix):
-    width = parts[0].shape[1] - LANES
-    stats = [part[:, width:] for part in parts]
-    peaks = [jnp.dot(s, peak_matrix, preferred_element_type=F32) for s in stats]
+def by_row(table, rows):
+    if table.shape[0] < LANES:
+        rest = jnp.zeros((LANES - table.shape[0], LANES), F32)
+        table = jnp.concatenate([table, rest], axis=0)
+    table = jnp.transpose(table)
+    odd = lax.rem(column(), 2)
+    return jnp.where(odd == 0, table[:rows], table[rows : 2 * rows])
+
+
+def head_columns(width):
+    shape = (LANES, width)
+    head = lax.broadcasted_iota(jnp.int32, shape, 1) // (width // HEADS)
+    same = lax.broadcasted_iota(jnp.int32, shape, 0) == head
+    return jnp.where(same, 1.0, 0.0).astype(BF16)
+
+
+def tree(terms):
+    while len(terms) > 1:
+        terms = [sum(terms[i : i + 2]) for i in range(0, len(terms), 2)]
+    return terms[0]
+
+
+def combine(refs):
+    rows, width = refs[0].shape[0] - HEADS, refs[0].shape[1]
+    stats = [ref[rows:].astype(F32) for ref in refs]
+    cut = lambda s, k: s[:, k * LANES : k * LANES + LANES]
+    peaks = [cut(s, 0) + cut(s, 1) + cut(s, 2) for s in stats]
     top = functools.reduce(jnp.maximum, peaks)
-    factors = [jnp.exp2(peak - top) for peak in peaks]
-    sums = [f[:, :width] * part[:, :width].astype(F32) for f, part in zip(factors, parts)]
-    totals = [
-        f * jnp.dot(s, total_matrix, preferred_element_type=F32) for f, s in zip(factors, stats)
-    ]
-
-    def tree(terms):
-        while len(terms) > 1:
-            terms = [sum(terms[i : i + 2]) for i in range(0, len(terms), 2)]
-        return terms[0]
-
-    return tree(sums), top, tree(totals)
-
-
-def packed(sums, top, total):
-    width = sums.shape[1]
-    return jnp.concatenate(
-        [sums.astype(BF16), pack_stats(top[:, width:], total[:, width:])], axis=1
-    )
-
-
-def merge_kernel(parts_ref, peak_ref, total_ref, out_ref):
-    parts = [parts_ref[i] for i in range(parts_ref.shape[0])]
-    out_ref[...] = packed(*combine(parts, peak_ref[...], total_ref[...]))
-
-
-def merge_two_kernel(a_ref, b_ref, peak_ref, total_ref, out_ref):
-    out_ref[...] = packed(*combine([a_ref[...], b_ref[...]], peak_ref[...], total_ref[...]))
+    factors = [jnp.exp2(peak - top).astype(BF16).astype(F32) for peak in peaks]
+    total = tree([f * cut(s, 3) for f, s in zip(factors, stats)])
+    table = by_row(jnp.concatenate(factors, axis=0), rows)
+    spread = head_columns(width)
+    sums = []
+    for i, ref in enumerate(refs):
+        factor = table if i == 0 else pltpu.roll(table, LANES - i * HEADS, 1)
+        factor = jnp.dot(factor.astype(BF16), spread, preferred_element_type=F32)
+        sums.append(factor * ref[:rows].astype(F32))
+    return tree(sums), top, total
+
+
+def write_merged(out_ref, sums, top, total):
+    rows = sums.shape[0]
+    out_ref[:rows] = sums.astype(BF16)
+    out_ref[rows:] = jnp.concatenate([*pieces(top), total], axis=1).astype(BF16)
+
+
+def merge_kernel(parts_ref, out_ref):
+    write_merged(out_ref, *combine([parts_ref.at[i] for i in range(parts_ref.shape[0])]))
+
+
+def merge_two_kernel(a_ref, b_ref, out_ref):
+    write_merged(out_ref, *combine([a_ref, b_ref]))
 
 
 def merge(kernel, shape, *operands):
@@ -292,8 +301,6 @@
     b_ref,
     c_ref,
     d_ref,
-    peak_ref,
-    total_ref,
     queries_hbm,
     proj_hbm,
     gain_ref,
@@ -305,9 +312,16 @@
     loads = start_all(
         ((proj_hbm.at[3], weights), (queries_hbm.at[column(), lax.axis_index("c")], queries)), sems
     )
-    parts = [ref[...] for ref in (a_ref, b_ref, c_ref, d_ref)]
-    sums, _, total = combine(parts, peak_ref[...], total_ref[...])
-    attended = (sums / total[:, : sums.shape[1]]).astype(BF16)
+    sums, _, total = combine([a_ref, b_ref, c_ref, d_ref])
+    rows, width = sums.shape
+    spread = head_columns(width)
+    total = tree(
+        [
+            jnp.dot(by_row(piece, rows).astype(BF16), spread, preferred_element_type=F32)
+            for piece in pieces(total)
+        ]
+    )
+    attended = (sums / total).astype(BF16)
     for load in loads:
         load.wait()
     crossed = jnp.dot(attended, weights[...], preferred_element_type=F32)
@@ -316,14 +330,13 @@
         out_ref[i] = first
 
 
-def first_state_of(parts, peak_matrix, total_matrix, queries, proj, gain, copies):
-    rows, full = parts[0].shape
-    width = full - LANES
+def first_state_of(parts, queries, proj, gain, copies):
+    rows, width = parts[0].shape[0] - HEADS, parts[0].shape[1]
     local = pl.BlockSpec(memory_space=pltpu.VMEM)
     hbm = pl.BlockSpec(memory_space=pltpu.HBM)
     return pl.pallas_call(
         first_kernel,
-        in_specs=[local] * 6 + [hbm, hbm, local],
+        in_specs=[local] * 4 + [hbm, hbm, local],
         out_specs=local,
         scratch_shapes=[
             pltpu.VMEM((rows, width), BF16),
@@ -335,8 +348,6 @@
         name="first_state",
     )(
         *parts,
-        peak_matrix,
-        total_matrix,
         queries.reshape(copies, 2, rows, width),
         proj,
         gain,
@@ -530,16 +541,14 @@
     swap = [(0, 1), (1, 0)]
     own = (patches, patch_level, patch_sheet)
     other = [lax.ppermute(array, "c", swap) for array in own]
-    spread = spread_matrices(queries.shape[1])
     parts = cross_partial(queries, query_pos, query_sheets, own, other, level_embed, cross_proj)
     parts = lax.all_to_all(parts, ("x", "y"), 0, 0, tiled=True)
-    part = merge(merge_kernel, parts.shape[1:], parts, *spread)
+    part = merge(merge_kernel, parts.shape[1:], parts)
     part = merge(
         merge_two_kernel,
         part.shape,
         part,
         lax.ppermute(part, "z", [(i, i ^ 1) for i in range(bands)]),
-        *spread,
     )
     sign = lambda i: 1 - 2 * (i % 2)
     shift = lambda hop: lax.ppermute(
@@ -548,7 +557,6 @@
     near, middle, far = shift(-1), shift(-2), shift(-3)
     first = first_state_of(
         (part, far, near, middle),
-        *spread,
         queries,
         cross_proj,
         norm_gain,

time: 93.3 us -> 91.8 us (0.984)
  blocking collectives: 41.1 us -> 39.5 us
    all_to_all x1, blocking collectives: 24.2 us -> 22.8 us  [body(): parts = lax.all_to_all(parts, ('x', 'y'), 0, 0, tiled=True)]
where the time goes in v3:
time: 91.8 us; the launch traced here: 91.6 us
  blocking collectives  39.5 us (43%)
  Pallas kernels  24.9 us (27%)
  starting transfers between devices  18.6 us (20%)
  waiting for transfers between devices  7.2 us (8%)
    all_to_all x1, blocking collectives, body(): parts = lax.all_to_all(parts, ('x', 'y'), 0, 0, tiled=True)  22.8 us
    all_to_all x1, blocking collectives, body(): own = lax.all_to_all(first, ('x', 'y'), 0, 0, tiled=True)  16.8 us
    pallas_call x1, Pallas kernels, cross_partial(): pl.pallas_call(cross_kernel, in_specs=[hbm] * 11, out_specs=hbm, scratch_...  15.1 us
    ppermute x3, starting transfers between devices, body(): lax.ppermute(part, 'z', [(i, (i + hop * sign(i)) % bands) for i in range(...  8.27 us
    pallas_call x1, Pallas kernels, tail(): pl.pallas_call(tail_kernel, in_specs=[local] * 5 + [hbm] * 4 + [local], o...  5.28 us
    ppermute x1, starting transfers between devices, body(): other = lax.ppermute(own, 'c', swap)  4.88 us
    ppermute x3, waiting for transfers between devices, body(): lax.ppermute(part, 'z', [(i, (i + hop * sign(i)) % bands) for i in range(...  4.21 us
    ppermute x3, starting transfers between devices, body(): other = [lax.ppermute(array, 'c', swap) for array in own]  3.75 us
  transfers between devices with their start and end apart: 8, of which 4 were waited for; matrix products, arithmetic and copies ran while one was open for 0% of the time, Pallas kernels for 3%

profile of v3, /device:TPU:1, one launch (start us, length us, event | category | flops | bytes accessed | tf_op | source)
XLA Modules:
  0.0 91.6 jit_solution(18353679789585015221)
XLA Ops:
  0.0 3.2 %collective-permute-start.2 = (bf16[512,512]{1,0:T(8,128)(2,1)}, bf16[512,512]{1,0:T(8,128)(2,1)S(1)}, u32[]{:S(2)}, u32[]{:S(2)}) collective-permute-start(bf16[512,512]{1,0:T(8,128)(2,1)} %patch_a_hbm.1), channel_id=1, source_target_pairs={{0,1},{1,0},{2,3},{3,2},{4,5},{5,4},{6,7},{7,6},{8,9},{9,8},{10,11... | collective-permute-start | bytes 1572872 | tf_op jit(solution)/shard_map/ppermute | solution.py:543
  3.2 0.0 collective-permute-start
  3.2 0.5 collective-permute-start.1
  3.8 1.2 %collective-permute-done.level_b_hbm = s32[512]{0:T(512)S(1)} collective-permute-done((s32[512]{0:T(512)}, s32[512]{0:T(512)S(1)}, u32[]{:S(2)}, u32[]{:S(2)}) %collective-permute-start) | collective-permute-done | bytes 2080 | tf_op jit(solution)/shard_map/ppermute | solution.py:543
  5.0 0.0 copy-start.8
  5.0 0.0 collective-permute-done.1.sheet_b_hbm
  5.0 0.0 copy-start.9
  5.0 0.0 collective-permute-done.2.patch_b_hbm
  5.0 0.0 copy-start.7
  5.0 0.6 copy-done.8
  5.6 0.0 copy-done.9
  5.6 0.2 copy-done.7
  5.8 0.0 copy-start.1
  5.8 15.1 %cross_partial.1 = bf16[16,72,512]{2,1,0:T(8,128)(2,1)} custom-call(s32[512]{0:T(512)} %level_a_hbm.1, s32[512]{0:T(512)} %sheet_a_hbm.1, s32[512]{0:T(512)} %copy-done.8, s32[512]{0:T(512)} %copy-done.9, bf16[4,512]{1,0:T(4,128)(2,1)} %level_hbm.1, s32[16,2048]{1,0:T(8,128)} %bitcast.8, bf16[512,512]{1,0:T(8,128)(2,1)} %patch_a_hbm.1, ...), custom_call_target="tpu_custom_call" | custom-call | tf_op jit(solution)/shard_map/cross_partial/pallas_call | solution.py:197
  21.1 0.0 copy-start
  21.2 0.0 copy-start.6
  21.2 22.8 %all_to_all.10.parts_ref = bf16[16,72,512]{2,1,0:T(8,128)(2,1)S(1)} all-to-all(bf16[16,72,512]{2,1,0:T(8,128)(2,1)} %cross_partial.1), channel_id=1, replica_groups=mesh['z'=8,'x'=4,'y'=4,'c'=2] {'x','y'}, dimensions={0} | all-to-all | bytes 2359296 | tf_op jit(solution)/shard_map/all_to_all | solution.py:545
  43.9 0.6 merge.2.a_ref
  44.5 1.7 %collective-permute-start.3 = (bf16[72,512]{1,0:T(8,128)(2,1)S(1)}, bf16[72,512]{1,0:T(8,128)(2,1)S(1)}, u32[]{:S(2)}, u32[]{:S(2)}) collective-permute-start(bf16[72,512]{1,0:T(8,128)(2,1)S(1)} %merge.2.a_ref), channel_id=1, source_target_pairs={{0,32},{32,0},{64,96},{96,64},{128,160},{160,128},{192,224},{224,1... | collective-permute-start | bytes 221192 | tf_op jit(solution)/shard_map/ppermute | solution.py:551
  46.3 1.7 %collective-permute-done.3.b_ref = bf16[72,512]{1,0:T(8,128)(2,1)S(1)} collective-permute-done((bf16[72,512]{1,0:T(8,128)(2,1)S(1)}, bf16[72,512]{1,0:T(8,128)(2,1)S(1)}, u32[]{:S(2)}, u32[]{:S(2)}) %collective-permute-start.3) | collective-permute-done | bytes 73760 | tf_op jit(solution)/shard_map/ppermute | solution.py:551
  48.0 0.3 merge.3.a_ref
  48.3 5.9 %collective-permute-start.6 = (bf16[72,512]{1,0:T(8,128)(2,1)S(1)}, bf16[72,512]{1,0:T(8,128)(2,1)S(1)}, u32[]{:S(2)}, u32[]{:S(2)}) collective-permute-start(bf16[72,512]{1,0:T(8,128)(2,1)S(1)} %merge.3.a_ref), channel_id=1, source_target_pairs={{0,192},{32,96},{64,0},{96,160},{128,64},{160,224},{192,128},{224,... | collective-permute-start | bytes 221192 | tf_op jit(solution)/shard_map/ppermute | solution.py:554
  54.3 0.0 collective-permute-start.5
  54.3 2.4 %collective-permute-start.4 = (bf16[72,512]{1,0:T(8,128)(2,1)S(1)}, bf16[72,512]{1,0:T(8,128)(2,1)S(1)}, u32[]{:S(2)}, u32[]{:S(2)}) collective-permute-start(bf16[72,512]{1,0:T(8,128)(2,1)S(1)} %merge.3.a_ref), channel_id=1, source_target_pairs={{0,160},{32,128},{64,224},{96,192},{128,32},{160,0},{192,96},{224,... | collective-permute-start | bytes 221192 | tf_op jit(solution)/shard_map/ppermute | solution.py:554
  56.6 0.0 collective-permute-done.6.d_ref
  56.6 2.8 %collective-permute-done.5.c_ref = bf16[72,512]{1,0:T(8,128)(2,1)S(1)} collective-permute-done((bf16[72,512]{1,0:T(8,128)(2,1)S(1)}, bf16[72,512]{1,0:T(8,128)(2,1)S(1)}, u32[]{:S(2)}, u32[]{:S(2)}) %collective-permute-start.5) | collective-permute-done | bytes 73760 | tf_op jit(solution)/shard_map/ppermute | solution.py:554
  59.4 1.4 %collective-permute-done.4.b_ref = bf16[72,512]{1,0:T(8,128)(2,1)S(1)} collective-permute-done((bf16[72,512]{1,0:T(8,128)(2,1)S(1)}, bf16[72,512]{1,0:T(8,128)(2,1)S(1)}, u32[]{:S(2)}, u32[]{:S(2)}) %collective-permute-start.4) | collective-permute-done | bytes 73760 | tf_op jit(solution)/shard_map/ppermute | solution.py:554
  60.8 0.0 copy-done.1
  60.8 0.0 copy-done
  60.8 0.0 copy-done.6
  60.8 0.0 copy-start.3
  60.9 1.1 %first_state.1.first_ref = bf16[16,64,512]{2,1,0:T(8,128)(2,1)S(1)} custom-call(bf16[72,512]{1,0:T(8,128)(2,1)S(1)} %merge.3.a_ref, bf16[72,512]{1,0:T(8,128)(2,1)S(1)} %collective-permute-done.4.b_ref, bf16[72,512]{1,0:T(8,128)(2,1)S(1)} %collective-permute-done.5.c_ref, bf16[72,512]{1,0:T(8,128)(2,1)S(1)} %collective-permute-done.6.d_ref, ...), custom_call_target="tpu_custom_call" | custom-call | tf_op jit(solution)/shard_map/first_state/pallas_call | solution.py:337
  61.9 0.0 copy-start.2
  62.0 16.8 %all_to_all.11.state_ref = bf16[16,64,512]{2,1,0:T(8,128)(2,1)S(1)} all-to-all(bf16[16,64,512]{2,1,0:T(8,128)(2,1)S(1)} %first_state.1.first_ref), channel_id=1, replica_groups=mesh['z'=8,'x'=4,'y'=4,'c'=2] {'x','y'}, dimensions={0} | all-to-all | bytes 2097152 | tf_op jit(solution)/shard_map/all_to_all | solution.py:565
  78.7 0.0 copy-start.4
  78.7 0.0 copy-start.5
  78.7 4.9 %collective-permute-start.7 = (bf16[16,64,512]{2,1,0:T(8,128)(2,1)S(1)}, bf16[16,64,512]{2,1,0:T(8,128)(2,1)S(1)}, u32[]{:S(2)}, u32[]{:S(2)}) collective-permute-start(bf16[16,64,512]{2,1,0:T(8,128)(2,1)S(1)} %all_to_all.11.state_ref), channel_id=1, source_target_pairs={{0,1},{1,0},{2,3},{3,2},{4,5},{5,4},{6,7},{7,6},{8,9},{9,8},{10,11... | collective-permute-start | bytes 3145736 | tf_op jit(solution)/shard_map/ppermute | solution.py:566
  83.6 0.0 copy-done.3
  83.6 0.0 copy-done.2
  83.6 2.5 %near_half.1 = (bf16[512,512]{1,0:T(8,128)(2,1)S(1)}, f32[512,512]{1,0:T(8,128)S(1)}, f32[512,128]{1,0:T(8,128)S(1)}) custom-call(bf16[16,64,512]{2,1,0:T(8,128)(2,1)S(1)} %first_state.1.first_ref, bf16[16,64,512]{2,1,0:T(8,128)(2,1)S(1)} %all_to_all.11.state_ref, bf16[16,2,64,512]{3,2,1,0:T(8,128)(2,1)S(1)} %bitcast.6, bf16[4,512,512]{2,1,0:T(8,128)(2,1)S(1)} %copy-done.3), custom_call_target="tpu_custom_call" | custom-call | flops 8589934592 | bytes 4194304 | tf_op jit(solution)/shard_map/near_half/pallas_call | solution.py:413
  86.1 0.0 collective-permute-done.7.state_ref
  86.1 0.0 copy-done.4
  86.1 0.0 copy-done.5
  86.1 5.3 %tail.1 = bf16[64,512]{1,0:T(8,128)(2,1)} custom-call(bf16[16,64,512]{2,1,0:T(8,128)(2,1)S(1)} %first_state.1.first_ref, bf16[512,512]{1,0:T(8,128)(2,1)S(1)} %get-tuple-element.8.absorbed_ref, f32[512,512]{1,0:T(8,128)S(1)} %get-tuple-element.9.mixed_ref, f32[512,128]{1,0:T(8,128)S(1)} %get-tuple-element.10.stat_ref, ...), custom_call_target="tpu_custom_call" | custom-call | tf_op jit(solution)/shard_map/tail/pallas_call | solution.py:499
Async XLA Ops:
  0.0 5.0 %collective-permute-start.2 = (bf16[512,512]{1,0:T(8,128)(2,1)}, bf16[512,512]{1,0:T(8,128)(2,1)S(1)}, u32[]{:S(2)}, u32[]{:S(2)}) collective-permute-start(bf16[512,512]{1,0:T(8,128)(2,1)} %patch_a_hbm.1), channel_id=1, source_target_pairs={{0,1},{1,0},{2,3},{3,2},{4,5},{5,4},{6,7},{7,6},{8,9},{9,8},{10,11... | collective-permute-start | bytes 1572872 | tf_op jit(solution)/shard_map/ppermute | solution.py:543
  3.2 1.8 %collective-permute-start = (s32[512]{0:T(512)}, s32[512]{0:T(512)S(1)}, u32[]{:S(2)}, u32[]{:S(2)}) collective-permute-start(s32[512]{0:T(512)} %level_a_hbm.1), channel_id=1, source_target_pairs={{0,1},{1,0},{2,3},{3,2},{4,5},{5,4},{6,7},{7,6},{8,9},{9,8},{10,11... | collective-permute-start | bytes 6152 | tf_op jit(solution)/shard_map/ppermute | solution.py:543
  3.2 1.8 %collective-permute-start.1 = (s32[512]{0:T(512)}, s32[512]{0:T(512)S(1)}, u32[]{:S(2)}, u32[]{:S(2)}) collective-permute-start(s32[512]{0:T(512)} %sheet_a_hbm.1), channel_id=1, source_target_pairs={{0,1},{1,0},{2,3},{3,2},{4,5},{5,4},{6,7},{7,6},{8,9},{9,8},{10,11... | collective-permute-start | bytes 6152 | tf_op jit(solution)/shard_map/ppermute | solution.py:543
  5.0 0.6 copy-start.8
  5.0 0.6 copy-start.9
  5.0 0.8 copy-start.7
  5.8 55.0 %copy-start.1 = (bf16[4,512,512]{2,1,0:T(8,128)(2,1)S(1)}, bf16[4,512,512]{2,1,0:T(8,128)(2,1)}, u32[]{:S(2)}) copy-start(bf16[4,512,512]{2,1,0:T(8,128)(2,1)} %proj_hbm.5) | copy-start | bytes 6291460
  21.1 39.7 %copy-start = (bf16[2048,512]{1,0:T(8,128)(2,1)S(1)}, bf16[2048,512]{1,0:T(8,128)(2,1)}, u32[]{:S(2)}) copy-start(bf16[2048,512]{1,0:T(8,128)(2,1)} %param.12) | copy-start | bytes 6291460
  21.2 39.7 %copy-start.6 = (f32[3,512]{1,0:T(4,128)S(1)}, f32[3,512]{1,0:T(4,128)}, u32[]{:S(2)}) copy-start(f32[3,512]{1,0:T(4,128)} %gain_ref.3) | copy-start | bytes 18436
  44.5 3.5 %collective-permute-start.3 = (bf16[72,512]{1,0:T(8,128)(2,1)S(1)}, bf16[72,512]{1,0:T(8,128)(2,1)S(1)}, u32[]{:S(2)}, u32[]{:S(2)}) collective-permute-start(bf16[72,512]{1,0:T(8,128)(2,1)S(1)} %merge.2.a_ref), channel_id=1, source_target_pairs={{0,32},{32,0},{64,96},{96,64},{128,160},{160,128},{192,224},{224,1... | collective-permute-start | bytes 221192 | tf_op jit(solution)/shard_map/ppermute | solution.py:551
  48.3 8.3 %collective-permute-start.6 = (bf16[72,512]{1,0:T(8,128)(2,1)S(1)}, bf16[72,512]{1,0:T(8,128)(2,1)S(1)}, u32[]{:S(2)}, u32[]{:S(2)}) collective-permute-start(bf16[72,512]{1,0:T(8,128)(2,1)S(1)} %merge.3.a_ref), channel_id=1, source_target_pairs={{0,192},{32,96},{64,0},{96,160},{128,64},{160,224},{192,128},{224,... | collective-permute-start | bytes 221192 | tf_op jit(solution)/shard_map/ppermute | solution.py:554
  54.3 5.2 %collective-permute-start.5 = (bf16[72,512]{1,0:T(8,128)(2,1)S(1)}, bf16[72,512]{1,0:T(8,128)(2,1)S(1)}, u32[]{:S(2)}, u32[]{:S(2)}) collective-permute-start(bf16[72,512]{1,0:T(8,128)(2,1)S(1)} %merge.3.a_ref), channel_id=1, source_target_pairs={{0,224},{32,64},{64,32},{96,128},{128,96},{160,192},{192,160},{224... | collective-permute-start | bytes 221192 | tf_op jit(solution)/shard_map/ppermute | solution.py:554
  54.3 6.6 %collective-permute-start.4 = (bf16[72,512]{1,0:T(8,128)(2,1)S(1)}, bf16[72,512]{1,0:T(8,128)(2,1)S(1)}, u32[]{:S(2)}, u32[]{:S(2)}) collective-permute-start(bf16[72,512]{1,0:T(8,128)(2,1)S(1)} %merge.3.a_ref), channel_id=1, source_target_pairs={{0,160},{32,128},{64,224},{96,192},{128,32},{160,0},{192,96},{224,... | collective-permute-start | bytes 221192 | tf_op jit(solution)/shard_map/ppermute | solution.py:554
  60.8 22.8 %copy-start.3 = (bf16[4,512,512]{2,1,0:T(8,128)(2,1)S(1)}, bf16[4,512,512]{2,1,0:T(8,128)(2,1)}, u32[]{:S(2)}) copy-start(bf16[4,512,512]{2,1,0:T(8,128)(2,1)} %proj_hbm.7) | copy-start | bytes 6291460
  61.9 21.7 %copy-start.2 = (bf16[2048,512]{1,0:T(8,128)(2,1)S(1)}, bf16[2048,512]{1,0:T(8,128)(2,1)}, u32[]{:S(2)}) copy-start(bf16[2048,512]{1,0:T(8,128)(2,1)} %param.13) | copy-start | bytes 6291460
  78.7 7.4 %copy-start.4 = (bf16[512,2048]{1,0:T(8,128)(2,1)S(1)}, bf16[512,2048]{1,0:T(8,128)(2,1)}, u32[]{:S(2)}) copy-start(bf16[512,2048]{1,0:T(8,128)(2,1)} %mlp_in_hbm.1) | copy-start | bytes 6291460
  78.7 7.4 %copy-start.5 = (bf16[2048,512]{1,0:T(8,128)(2,1)S(1)}, bf16[2048,512]{1,0:T(8,128)(2,1)}, u32[]{:S(2)}) copy-start(bf16[2048,512]{1,0:T(8,128)(2,1)} %mlp_out_hbm.1) | copy-start | bytes 6291460
  78.7 7.4 %collective-permute-start.7 = (bf16[16,64,512]{2,1,0:T(8,128)(2,1)S(1)}, bf16[16,64,512]{2,1,0:T(8,128)(2,1)S(1)}, u32[]{:S(2)}, u32[]{:S(2)}) collective-permute-start(bf16[16,64,512]{2,1,0:T(8,128)(2,1)S(1)} %all_to_all.11.state_ref), channel_id=1, source_target_pairs={{0,1},{1,0},{2,3},{3,2},{4,5},{5,4},{6,7},{7,6},{8,9},{9,8},{10,11... | collective-permute-start | bytes 3145736 | tf_op jit(solution)/shard_map/ppermute | solution.py:566

commit v4 on v3

--- a/solution.py
+++ b/solution.py
@@ -312,7 +312,7 @@
     loads = start_all(
         ((proj_hbm.at[3], weights), (queries_hbm.at[column(), lax.axis_index("c")], queries)), sems
     )
-    sums, _, total = combine([a_ref, b_ref, c_ref, d_ref])
+    sums, _, total = combine([a_ref, d_ref, b_ref, c_ref])
     rows, width = sums.shape
     spread = head_columns(width)
     total = tree(
@@ -556,7 +556,7 @@
     )
     near, middle, far = shift(-1), shift(-2), shift(-3)
     first = first_state_of(
-        (part, far, near, middle),
+        (part, near, middle, far),
         queries,
         cross_proj,
         norm_gain,

time: 91.8 us -> 91.7 us (level)
  starting transfers between devices: 18.6 us -> 19.9 us
  waiting for transfers between devices: 7.2 us -> 6.23 us
    ppermute x3, starting transfers between devices: 8.27 us -> 9.49 us  [body(): lax.ppermute(part, 'z', [(i, (i + hop * sign(i)) % bands) for i in range(...]
    ppermute x3, waiting for transfers between devices: 4.21 us -> 3.24 us  [body(): lax.ppermute(part, 'z', [(i, (i + hop * sign(i)) % bands) for i in range(...]
where the time goes in v4:
time: 91.7 us; the launch traced here: 91.5 us
  blocking collectives  39.1 us (43%)
  Pallas kernels  24.9 us (27%)
  starting transfers between devices  19.9 us (22%)
  waiting for transfers between devices  6.23 us (7%)
    all_to_all x1, blocking collectives, body(): parts = lax.all_to_all(parts, ('x', 'y'), 0, 0, tiled=True)  22.8 us
    all_to_all x1, blocking collectives, body(): own = lax.all_to_all(first, ('x', 'y'), 0, 0, tiled=True)  16.4 us
    pallas_call x1, Pallas kernels, cross_partial(): pl.pallas_call(cross_kernel, in_specs=[hbm] * 11, out_specs=hbm, scratch_...  15.1 us
    ppermute x3, starting transfers between devices, body(): lax.ppermute(part, 'z', [(i, (i + hop * sign(i)) % bands) for i in range(...  9.49 us
    pallas_call x1, Pallas kernels, tail(): pl.pallas_call(tail_kernel, in_specs=[local] * 5 + [hbm] * 4 + [local], o...  5.28 us
    ppermute x1, starting transfers between devices, body(): other = lax.ppermute(own, 'c', swap)  4.94 us
    ppermute x3, starting transfers between devices, body(): other = [lax.ppermute(array, 'c', swap) for array in own]  3.75 us
    ppermute x3, waiting for transfers between devices, body(): lax.ppermute(part, 'z', [(i, (i + hop * sign(i)) % bands) for i in range(...  3.24 us
  transfers between devices with their start and end apart: 8, of which 4 were waited for; matrix products, arithmetic and copies ran while one was open for 0% of the time, Pallas kernels for 3%

profile of v4, /device:TPU:1, one launch (start us, length us, event | category | flops | bytes accessed | tf_op | source)
XLA Modules:
  0.0 91.5 jit_solution(4973973118548394461)
XLA Ops:
  0.0 3.2 %collective-permute-start.2 = (bf16[512,512]{1,0:T(8,128)(2,1)}, bf16[512,512]{1,0:T(8,128)(2,1)S(1)}, u32[]{:S(2)}, u32[]{:S(2)}) collective-permute-start(bf16[512,512]{1,0:T(8,128)(2,1)} %patch_a_hbm.1), channel_id=1, source_target_pairs={{0,1},{1,0},{2,3},{3,2},{4,5},{5,4},{6,7},{7,6},{8,9},{9,8},{10,11... | collective-permute-start | bytes 1572872 | tf_op jit(solution)/shard_map/ppermute | solution.py:543
  3.2 0.0 collective-permute-start
  3.2 0.5 collective-permute-start.1
  3.8 1.2 %collective-permute-done.level_b_hbm = s32[512]{0:T(512)S(1)} collective-permute-done((s32[512]{0:T(512)}, s32[512]{0:T(512)S(1)}, u32[]{:S(2)}, u32[]{:S(2)}) %collective-permute-start) | collective-permute-done | bytes 2080 | tf_op jit(solution)/shard_map/ppermute | solution.py:543
  5.0 0.0 copy-start.8
  5.0 0.0 collective-permute-done.1.sheet_b_hbm
  5.0 0.0 copy-start.9
  5.0 0.0 collective-permute-done.2.patch_b_hbm
  5.0 0.0 copy-start.7
  5.0 0.6 copy-done.8
  5.6 0.0 copy-done.9
  5.6 0.2 copy-done.7
  5.8 0.0 copy-start.1
  5.8 15.1 %cross_partial.1 = bf16[16,72,512]{2,1,0:T(8,128)(2,1)} custom-call(s32[512]{0:T(512)} %level_a_hbm.1, s32[512]{0:T(512)} %sheet_a_hbm.1, s32[512]{0:T(512)} %copy-done.8, s32[512]{0:T(512)} %copy-done.9, bf16[4,512]{1,0:T(4,128)(2,1)} %level_hbm.1, s32[16,2048]{1,0:T(8,128)} %bitcast.8, bf16[512,512]{1,0:T(8,128)(2,1)} %patch_a_hbm.1, ...), custom_call_target="tpu_custom_call" | custom-call | tf_op jit(solution)/shard_map/cross_partial/pallas_call | solution.py:197
  21.1 0.0 copy-start
  21.2 0.0 copy-start.6
  21.2 22.8 %all_to_all.10.parts_ref = bf16[16,72,512]{2,1,0:T(8,128)(2,1)S(1)} all-to-all(bf16[16,72,512]{2,1,0:T(8,128)(2,1)} %cross_partial.1), channel_id=1, replica_groups=mesh['z'=8,'x'=4,'y'=4,'c'=2] {'x','y'}, dimensions={0} | all-to-all | bytes 2359296 | tf_op jit(solution)/shard_map/all_to_all | solution.py:545
  43.9 0.6 merge.2.a_ref
  44.5 1.7 %collective-permute-start.3 = (bf16[72,512]{1,0:T(8,128)(2,1)S(1)}, bf16[72,512]{1,0:T(8,128)(2,1)S(1)}, u32[]{:S(2)}, u32[]{:S(2)}) collective-permute-start(bf16[72,512]{1,0:T(8,128)(2,1)S(1)} %merge.2.a_ref), channel_id=1, source_target_pairs={{0,32},{32,0},{64,96},{96,64},{128,160},{160,128},{192,224},{224,1... | collective-permute-start | bytes 221192 | tf_op jit(solution)/shard_map/ppermute | solution.py:551
  46.3 1.7 %collective-permute-done.3.b_ref = bf16[72,512]{1,0:T(8,128)(2,1)S(1)} collective-permute-done((bf16[72,512]{1,0:T(8,128)(2,1)S(1)}, bf16[72,512]{1,0:T(8,128)(2,1)S(1)}, u32[]{:S(2)}, u32[]{:S(2)}) %collective-permute-start.3) | collective-permute-done | bytes 73760 | tf_op jit(solution)/shard_map/ppermute | solution.py:551
  48.0 0.3 merge.3.a_ref
  48.3 6.4 %collective-permute-start.6 = (bf16[72,512]{1,0:T(8,128)(2,1)S(1)}, bf16[72,512]{1,0:T(8,128)(2,1)S(1)}, u32[]{:S(2)}, u32[]{:S(2)}) collective-permute-start(bf16[72,512]{1,0:T(8,128)(2,1)S(1)} %merge.3.a_ref), channel_id=1, source_target_pairs={{0,160},{32,128},{64,224},{96,192},{128,32},{160,0},{192,96},{224,... | collective-permute-start | bytes 221192 | tf_op jit(solution)/shard_map/ppermute | solution.py:554
  54.7 0.3 collective-permute-start.5
  55.0 2.9 %collective-permute-start.4 = (bf16[72,512]{1,0:T(8,128)(2,1)S(1)}, bf16[72,512]{1,0:T(8,128)(2,1)S(1)}, u32[]{:S(2)}, u32[]{:S(2)}) collective-permute-start(bf16[72,512]{1,0:T(8,128)(2,1)S(1)} %merge.3.a_ref), channel_id=1, source_target_pairs={{0,224},{32,64},{64,32},{96,128},{128,96},{160,192},{192,160},{224... | collective-permute-start | bytes 221192 | tf_op jit(solution)/shard_map/ppermute | solution.py:554
  57.8 0.0 collective-permute-done.6.d_ref
  57.8 1.3 %collective-permute-done.5.c_ref = bf16[72,512]{1,0:T(8,128)(2,1)S(1)} collective-permute-done((bf16[72,512]{1,0:T(8,128)(2,1)S(1)}, bf16[72,512]{1,0:T(8,128)(2,1)S(1)}, u32[]{:S(2)}, u32[]{:S(2)}) %collective-permute-start.5) | collective-permute-done | bytes 73760 | tf_op jit(solution)/shard_map/ppermute | solution.py:554
  59.1 2.0 %collective-permute-done.4.b_ref = bf16[72,512]{1,0:T(8,128)(2,1)S(1)} collective-permute-done((bf16[72,512]{1,0:T(8,128)(2,1)S(1)}, bf16[72,512]{1,0:T(8,128)(2,1)S(1)}, u32[]{:S(2)}, u32[]{:S(2)}) %collective-permute-start.4) | collective-permute-done | bytes 73760 | tf_op jit(solution)/shard_map/ppermute | solution.py:554
  61.1 0.0 copy-done.1
  61.1 0.0 copy-done
  61.1 0.0 copy-done.6
  61.1 0.0 copy-start.3
  61.1 1.1 %first_state.1.first_ref = bf16[16,64,512]{2,1,0:T(8,128)(2,1)S(1)} custom-call(bf16[72,512]{1,0:T(8,128)(2,1)S(1)} %merge.3.a_ref, bf16[72,512]{1,0:T(8,128)(2,1)S(1)} %collective-permute-done.4.b_ref, bf16[72,512]{1,0:T(8,128)(2,1)S(1)} %collective-permute-done.5.c_ref, bf16[72,512]{1,0:T(8,128)(2,1)S(1)} %collective-permute-done.6.d_ref, ...), custom_call_target="tpu_custom_call" | custom-call | tf_op jit(solution)/shard_map/first_state/pallas_call | solution.py:337
  62.2 0.0 copy-start.2
  62.2 16.4 %all_to_all.11.state_ref = bf16[16,64,512]{2,1,0:T(8,128)(2,1)S(1)} all-to-all(bf16[16,64,512]{2,1,0:T(8,128)(2,1)S(1)} %first_state.1.first_ref), channel_id=1, replica_groups=mesh['z'=8,'x'=4,'y'=4,'c'=2] {'x','y'}, dimensions={0} | all-to-all | bytes 2097152 | tf_op jit(solution)/shard_map/all_to_all | solution.py:565
  78.6 0.0 copy-start.4
  78.6 0.0 copy-start.5
  78.6 4.9 %collective-permute-start.7 = (bf16[16,64,512]{2,1,0:T(8,128)(2,1)S(1)}, bf16[16,64,512]{2,1,0:T(8,128)(2,1)S(1)}, u32[]{:S(2)}, u32[]{:S(2)}) collective-permute-start(bf16[16,64,512]{2,1,0:T(8,128)(2,1)S(1)} %all_to_all.11.state_ref), channel_id=1, source_target_pairs={{0,1},{1,0},{2,3},{3,2},{4,5},{5,4},{6,7},{7,6},{8,9},{9,8},{10,11... | collective-permute-start | bytes 3145736 | tf_op jit(solution)/shard_map/ppermute | solution.py:566
  83.5 0.0 copy-done.3
  83.5 0.0 copy-done.2
  83.5 2.5 %near_half.1 = (bf16[512,512]{1,0:T(8,128)(2,1)S(1)}, f32[512,512]{1,0:T(8,128)S(1)}, f32[512,128]{1,0:T(8,128)S(1)}) custom-call(bf16[16,64,512]{2,1,0:T(8,128)(2,1)S(1)} %first_state.1.first_ref, bf16[16,64,512]{2,1,0:T(8,128)(2,1)S(1)} %all_to_all.11.state_ref, bf16[16,2,64,512]{3,2,1,0:T(8,128)(2,1)S(1)} %bitcast.6, bf16[4,512,512]{2,1,0:T(8,128)(2,1)S(1)} %copy-done.3), custom_call_target="tpu_custom_call" | custom-call | flops 8589934592 | bytes 4194304 | tf_op jit(solution)/shard_map/near_half/pallas_call | solution.py:413
  86.0 0.0 collective-permute-done.7.state_ref
  86.0 0.0 copy-done.4
  86.1 0.0 copy-done.5
  86.1 5.3 %tail.1 = bf16[64,512]{1,0:T(8,128)(2,1)} custom-call(bf16[16,64,512]{2,1,0:T(8,128)(2,1)S(1)} %first_state.1.first_ref, bf16[512,512]{1,0:T(8,128)(2,1)S(1)} %get-tuple-element.8.absorbed_ref, f32[512,512]{1,0:T(8,128)S(1)} %get-tuple-element.9.mixed_ref, f32[512,128]{1,0:T(8,128)S(1)} %get-tuple-element.10.stat_ref, ...), custom_call_target="tpu_custom_call" | custom-call | tf_op jit(solution)/shard_map/tail/pallas_call | solution.py:499
Async XLA Ops:
  0.0 5.0 %collective-permute-start.2 = (bf16[512,512]{1,0:T(8,128)(2,1)}, bf16[512,512]{1,0:T(8,128)(2,1)S(1)}, u32[]{:S(2)}, u32[]{:S(2)}) collective-permute-start(bf16[512,512]{1,0:T(8,128)(2,1)} %patch_a_hbm.1), channel_id=1, source_target_pairs={{0,1},{1,0},{2,3},{3,2},{4,5},{5,4},{6,7},{7,6},{8,9},{9,8},{10,11... | collective-permute-start | bytes 1572872 | tf_op jit(solution)/shard_map/ppermute | solution.py:543
  3.2 1.8 %collective-permute-start = (s32[512]{0:T(512)}, s32[512]{0:T(512)S(1)}, u32[]{:S(2)}, u32[]{:S(2)}) collective-permute-start(s32[512]{0:T(512)} %level_a_hbm.1), channel_id=1, source_target_pairs={{0,1},{1,0},{2,3},{3,2},{4,5},{5,4},{6,7},{7,6},{8,9},{9,8},{10,11... | collective-permute-start | bytes 6152 | tf_op jit(solution)/shard_map/ppermute | solution.py:543
  3.2 1.8 %collective-permute-start.1 = (s32[512]{0:T(512)}, s32[512]{0:T(512)S(1)}, u32[]{:S(2)}, u32[]{:S(2)}) collective-permute-start(s32[512]{0:T(512)} %sheet_a_hbm.1), channel_id=1, source_target_pairs={{0,1},{1,0},{2,3},{3,2},{4,5},{5,4},{6,7},{7,6},{8,9},{9,8},{10,11... | collective-permute-start | bytes 6152 | tf_op jit(solution)/shard_map/ppermute | solution.py:543
  5.0 0.6 copy-start.8
  5.0 0.6 copy-start.9
  5.0 0.8 copy-start.7
  5.8 55.3 %copy-start.1 = (bf16[4,512,512]{2,1,0:T(8,128)(2,1)S(1)}, bf16[4,512,512]{2,1,0:T(8,128)(2,1)}, u32[]{:S(2)}) copy-start(bf16[4,512,512]{2,1,0:T(8,128)(2,1)} %proj_hbm.5) | copy-start | bytes 6291460
  21.1 39.9 %copy-start = (bf16[2048,512]{1,0:T(8,128)(2,1)S(1)}, bf16[2048,512]{1,0:T(8,128)(2,1)}, u32[]{:S(2)}) copy-start(bf16[2048,512]{1,0:T(8,128)(2,1)} %param.12) | copy-start | bytes 6291460
  21.2 39.9 %copy-start.6 = (f32[3,512]{1,0:T(4,128)S(1)}, f32[3,512]{1,0:T(4,128)}, u32[]{:S(2)}) copy-start(f32[3,512]{1,0:T(4,128)} %gain_ref.3) | copy-start | bytes 18436
  44.5 3.5 %collective-permute-start.3 = (bf16[72,512]{1,0:T(8,128)(2,1)S(1)}, bf16[72,512]{1,0:T(8,128)(2,1)S(1)}, u32[]{:S(2)}, u32[]{:S(2)}) collective-permute-start(bf16[72,512]{1,0:T(8,128)(2,1)S(1)} %merge.2.a_ref), channel_id=1, source_target_pairs={{0,32},{32,0},{64,96},{96,64},{128,160},{160,128},{192,224},{224,1... | collective-permute-start | bytes 221192 | tf_op jit(solution)/shard_map/ppermute | solution.py:551
  48.3 9.5 %collective-permute-start.6 = (bf16[72,512]{1,0:T(8,128)(2,1)S(1)}, bf16[72,512]{1,0:T(8,128)(2,1)S(1)}, u32[]{:S(2)}, u32[]{:S(2)}) collective-permute-start(bf16[72,512]{1,0:T(8,128)(2,1)S(1)} %merge.3.a_ref), channel_id=1, source_target_pairs={{0,160},{32,128},{64,224},{96,192},{128,32},{160,0},{192,96},{224,... | collective-permute-start | bytes 221192 | tf_op jit(solution)/shard_map/ppermute | solution.py:554
  54.7 4.4 %collective-permute-start.5 = (bf16[72,512]{1,0:T(8,128)(2,1)S(1)}, bf16[72,512]{1,0:T(8,128)(2,1)S(1)}, u32[]{:S(2)}, u32[]{:S(2)}) collective-permute-start(bf16[72,512]{1,0:T(8,128)(2,1)S(1)} %merge.3.a_ref), channel_id=1, source_target_pairs={{0,192},{32,96},{64,0},{96,160},{128,64},{160,224},{192,128},{224,... | collective-permute-start | bytes 221192 | tf_op jit(solution)/shard_map/ppermute | solution.py:554
  55.0 6.1 %collective-permute-start.4 = (bf16[72,512]{1,0:T(8,128)(2,1)S(1)}, bf16[72,512]{1,0:T(8,128)(2,1)S(1)}, u32[]{:S(2)}, u32[]{:S(2)}) collective-permute-start(bf16[72,512]{1,0:T(8,128)(2,1)S(1)} %merge.3.a_ref), channel_id=1, source_target_pairs={{0,224},{32,64},{64,32},{96,128},{128,96},{160,192},{192,160},{224... | collective-permute-start | bytes 221192 | tf_op jit(solution)/shard_map/ppermute | solution.py:554
  61.1 22.5 %copy-start.3 = (bf16[4,512,512]{2,1,0:T(8,128)(2,1)S(1)}, bf16[4,512,512]{2,1,0:T(8,128)(2,1)}, u32[]{:S(2)}) copy-start(bf16[4,512,512]{2,1,0:T(8,128)(2,1)} %proj_hbm.7) | copy-start | bytes 6291460
  62.2 21.4 %copy-start.2 = (bf16[2048,512]{1,0:T(8,128)(2,1)S(1)}, bf16[2048,512]{1,0:T(8,128)(2,1)}, u32[]{:S(2)}) copy-start(bf16[2048,512]{1,0:T(8,128)(2,1)} %param.13) | copy-start | bytes 6291460
  78.6 7.4 %copy-start.4 = (bf16[512,2048]{1,0:T(8,128)(2,1)S(1)}, bf16[512,2048]{1,0:T(8,128)(2,1)}, u32[]{:S(2)}) copy-start(bf16[512,2048]{1,0:T(8,128)(2,1)} %mlp_in_hbm.1) | copy-start | bytes 6291460
  78.6 7.5 %copy-start.5 = (bf16[2048,512]{1,0:T(8,128)(2,1)S(1)}, bf16[2048,512]{1,0:T(8,128)(2,1)}, u32[]{:S(2)}) copy-start(bf16[2048,512]{1,0:T(8,128)(2,1)} %mlp_out_hbm.1) | copy-start | bytes 6291460
  78.6 7.4 %collective-permute-start.7 = (bf16[16,64,512]{2,1,0:T(8,128)(2,1)S(1)}, bf16[16,64,512]{2,1,0:T(8,128)(2,1)S(1)}, u32[]{:S(2)}, u32[]{:S(2)}) collective-permute-start(bf16[16,64,512]{2,1,0:T(8,128)(2,1)S(1)} %all_to_all.11.state_ref), channel_id=1, source_target_pairs={{0,1},{1,0},{2,3},{3,2},{4,5},{5,4},{6,7},{7,6},{8,9},{9,8},{10,11... | collective-permute-start | bytes 3145736 | tf_op jit(solution)/shard_map/ppermute | solution.py:566

commit v5 on v4

--- a/solution.py
+++ b/solution.py
@@ -556,7 +556,7 @@
     )
     near, middle, far = shift(-1), shift(-2), shift(-3)
     first = first_state_of(
-        (part, near, middle, far),
+        (part, middle, near, far),
         queries,
         cross_proj,
         norm_gain,

time: 91.7 us -> 90.9 us (level)
  starting transfers between devices: 19.9 us -> 17.1 us
  waiting for transfers between devices: 6.23 us -> 8.18 us
    ppermute x3, starting transfers between devices: 9.49 us -> 6.74 us  [body(): lax.ppermute(part, 'z', [(i, (i + hop * sign(i)) % bands) for i in range(...]
    ppermute x3, waiting for transfers between devices: 3.24 us -> 5.19 us  [body(): lax.ppermute(part, 'z', [(i, (i + hop * sign(i)) % bands) for i in range(...]
where the time goes in v5:
time: 90.9 us; the launch traced here: 90.7 us
  blocking collectives  39.2 us (43%)
  Pallas kernels  24.9 us (27%)
  starting transfers between devices  17.1 us (19%)
  waiting for transfers between devices  8.18 us (9%)
    all_to_all x1, blocking collectives, body(): parts = lax.all_to_all(parts, ('x', 'y'), 0, 0, tiled=True)  22.8 us
    all_to_all x1, blocking collectives, body(): own = lax.all_to_all(first, ('x', 'y'), 0, 0, tiled=True)  16.5 us
    pallas_call x1, Pallas kernels, cross_partial(): pl.pallas_call(cross_kernel, in_specs=[hbm] * 11, out_specs=hbm, scratch_...  15.1 us
    ppermute x3, starting transfers between devices, body(): lax.ppermute(part, 'z', [(i, (i + hop * sign(i)) % bands) for i in range(...  6.74 us
    pallas_call x1, Pallas kernels, tail(): pl.pallas_call(tail_kernel, in_specs=[local] * 5 + [hbm] * 4 + [local], o...  5.28 us
    ppermute x3, waiting for transfers between devices, body(): lax.ppermute(part, 'z', [(i, (i + hop * sign(i)) % bands) for i in range(...  5.19 us
    ppermute x1, starting transfers between devices, body(): other = lax.ppermute(own, 'c', swap)  4.84 us
    ppermute x3, starting transfers between devices, body(): other = [lax.ppermute(array, 'c', swap) for array in own]  3.75 us
  transfers between devices with their start and end apart: 8, of which 4 were waited for; matrix products, arithmetic and copies ran while one was open for 0% of the time, Pallas kernels for 3%

profile of v5, /device:TPU:1, one launch (start us, length us, event | category | flops | bytes accessed | tf_op | source)
XLA Modules:
  0.0 90.7 jit_solution(11535188573467278830)
XLA Ops:
  0.0 3.2 %collective-permute-start.2 = (bf16[512,512]{1,0:T(8,128)(2,1)}, bf16[512,512]{1,0:T(8,128)(2,1)S(1)}, u32[]{:S(2)}, u32[]{:S(2)}) collective-permute-start(bf16[512,512]{1,0:T(8,128)(2,1)} %patch_a_hbm.1), channel_id=1, source_target_pairs={{0,1},{1,0},{2,3},{3,2},{4,5},{5,4},{6,7},{7,6},{8,9},{9,8},{10,11... | collective-permute-start | bytes 1572872 | tf_op jit(solution)/shard_map/ppermute | solution.py:543
  3.2 0.0 collective-permute-start
  3.2 0.5 collective-permute-start.1
  3.8 1.2 %collective-permute-done.level_b_hbm = s32[512]{0:T(512)S(1)} collective-permute-done((s32[512]{0:T(512)}, s32[512]{0:T(512)S(1)}, u32[]{:S(2)}, u32[]{:S(2)}) %collective-permute-start) | collective-permute-done | bytes 2080 | tf_op jit(solution)/shard_map/ppermute | solution.py:543
  5.0 0.0 copy-start.8
  5.0 0.0 collective-permute-done.1.sheet_b_hbm
  5.0 0.0 copy-start.9
  5.0 0.0 collective-permute-done.2.patch_b_hbm
  5.0 0.0 copy-start.7
  5.0 0.6 copy-done.8
  5.6 0.0 copy-done.9
  5.6 0.2 copy-done.7
  5.8 0.0 copy-start.1
  5.8 15.1 %cross_partial.1 = bf16[16,72,512]{2,1,0:T(8,128)(2,1)} custom-call(s32[512]{0:T(512)} %level_a_hbm.1, s32[512]{0:T(512)} %sheet_a_hbm.1, s32[512]{0:T(512)} %copy-done.8, s32[512]{0:T(512)} %copy-done.9, bf16[4,512]{1,0:T(4,128)(2,1)} %level_hbm.1, s32[16,2048]{1,0:T(8,128)} %bitcast.8, bf16[512,512]{1,0:T(8,128)(2,1)} %patch_a_hbm.1, ...), custom_call_target="tpu_custom_call" | custom-call | tf_op jit(solution)/shard_map/cross_partial/pallas_call | solution.py:197
  21.1 0.0 copy-start
  21.2 0.0 copy-start.6
  21.2 22.8 %all_to_all.10.parts_ref = bf16[16,72,512]{2,1,0:T(8,128)(2,1)S(1)} all-to-all(bf16[16,72,512]{2,1,0:T(8,128)(2,1)} %cross_partial.1), channel_id=1, replica_groups=mesh['z'=8,'x'=4,'y'=4,'c'=2] {'x','y'}, dimensions={0} | all-to-all | bytes 2359296 | tf_op jit(solution)/shard_map/all_to_all | solution.py:545
  43.9 0.6 merge.2.a_ref
  44.5 1.7 %collective-permute-start.3 = (bf16[72,512]{1,0:T(8,128)(2,1)S(1)}, bf16[72,512]{1,0:T(8,128)(2,1)S(1)}, u32[]{:S(2)}, u32[]{:S(2)}) collective-permute-start(bf16[72,512]{1,0:T(8,128)(2,1)S(1)} %merge.2.a_ref), channel_id=1, source_target_pairs={{0,32},{32,0},{64,96},{96,64},{128,160},{160,128},{192,224},{224,1... | collective-permute-start | bytes 221192 | tf_op jit(solution)/shard_map/ppermute | solution.py:551
  46.3 1.7 %collective-permute-done.3.b_ref = bf16[72,512]{1,0:T(8,128)(2,1)S(1)} collective-permute-done((bf16[72,512]{1,0:T(8,128)(2,1)S(1)}, bf16[72,512]{1,0:T(8,128)(2,1)S(1)}, u32[]{:S(2)}, u32[]{:S(2)}) %collective-permute-start.3) | collective-permute-done | bytes 73760 | tf_op jit(solution)/shard_map/ppermute | solution.py:551
  48.0 0.3 merge.3.a_ref
  48.3 6.4 %collective-permute-start.6 = (bf16[72,512]{1,0:T(8,128)(2,1)S(1)}, bf16[72,512]{1,0:T(8,128)(2,1)S(1)}, u32[]{:S(2)}, u32[]{:S(2)}) collective-permute-start(bf16[72,512]{1,0:T(8,128)(2,1)S(1)} %merge.3.a_ref), channel_id=1, source_target_pairs={{0,160},{32,128},{64,224},{96,192},{128,32},{160,0},{192,96},{224,... | collective-permute-start | bytes 221192 | tf_op jit(solution)/shard_map/ppermute | solution.py:554
  54.7 0.0 collective-permute-start.5
  54.7 0.4 collective-permute-start.4
  55.1 1.4 %collective-permute-done.6.d_ref = bf16[72,512]{1,0:T(8,128)(2,1)S(1)} collective-permute-done((bf16[72,512]{1,0:T(8,128)(2,1)S(1)}, bf16[72,512]{1,0:T(8,128)(2,1)S(1)}, u32[]{:S(2)}, u32[]{:S(2)}) %collective-permute-start.6) | collective-permute-done | bytes 73760 | tf_op jit(solution)/shard_map/ppermute | solution.py:554
  56.4 3.8 %collective-permute-done.5.c_ref = bf16[72,512]{1,0:T(8,128)(2,1)S(1)} collective-permute-done((bf16[72,512]{1,0:T(8,128)(2,1)S(1)}, bf16[72,512]{1,0:T(8,128)(2,1)S(1)}, u32[]{:S(2)}, u32[]{:S(2)}) %collective-permute-start.5) | collective-permute-done | bytes 73760 | tf_op jit(solution)/shard_map/ppermute | solution.py:554
  60.3 0.0 collective-permute-done.4.b_ref
  60.3 0.0 copy-done.1
  60.3 0.0 copy-done
  60.3 0.0 copy-done.6
  60.3 0.0 copy-start.3
  60.3 1.1 %first_state.1.first_ref = bf16[16,64,512]{2,1,0:T(8,128)(2,1)S(1)} custom-call(bf16[72,512]{1,0:T(8,128)(2,1)S(1)} %merge.3.a_ref, bf16[72,512]{1,0:T(8,128)(2,1)S(1)} %collective-permute-done.4.b_ref, bf16[72,512]{1,0:T(8,128)(2,1)S(1)} %collective-permute-done.5.c_ref, bf16[72,512]{1,0:T(8,128)(2,1)S(1)} %collective-permute-done.6.d_ref, ...), custom_call_target="tpu_custom_call" | custom-call | tf_op jit(solution)/shard_map/first_state/pallas_call | solution.py:337
  61.4 0.0 copy-start.2
  61.4 16.5 %all_to_all.11.state_ref = bf16[16,64,512]{2,1,0:T(8,128)(2,1)S(1)} all-to-all(bf16[16,64,512]{2,1,0:T(8,128)(2,1)S(1)} %first_state.1.first_ref), channel_id=1, replica_groups=mesh['z'=8,'x'=4,'y'=4,'c'=2] {'x','y'}, dimensions={0} | all-to-all | bytes 2097152 | tf_op jit(solution)/shard_map/all_to_all | solution.py:565
  77.9 0.0 copy-start.4
  77.9 0.0 copy-start.5
  77.9 4.8 %collective-permute-start.7 = (bf16[16,64,512]{2,1,0:T(8,128)(2,1)S(1)}, bf16[16,64,512]{2,1,0:T(8,128)(2,1)S(1)}, u32[]{:S(2)}, u32[]{:S(2)}) collective-permute-start(bf16[16,64,512]{2,1,0:T(8,128)(2,1)S(1)} %all_to_all.11.state_ref), channel_id=1, source_target_pairs={{0,1},{1,0},{2,3},{3,2},{4,5},{5,4},{6,7},{7,6},{8,9},{9,8},{10,11... | collective-permute-start | bytes 3145736 | tf_op jit(solution)/shard_map/ppermute | solution.py:566
  82.7 0.0 copy-done.3
  82.7 0.0 copy-done.2
  82.7 2.5 %near_half.1 = (bf16[512,512]{1,0:T(8,128)(2,1)S(1)}, f32[512,512]{1,0:T(8,128)S(1)}, f32[512,128]{1,0:T(8,128)S(1)}) custom-call(bf16[16,64,512]{2,1,0:T(8,128)(2,1)S(1)} %first_state.1.first_ref, bf16[16,64,512]{2,1,0:T(8,128)(2,1)S(1)} %all_to_all.11.state_ref, bf16[16,2,64,512]{3,2,1,0:T(8,128)(2,1)S(1)} %bitcast.6, bf16[4,512,512]{2,1,0:T(8,128)(2,1)S(1)} %copy-done.3), custom_call_target="tpu_custom_call" | custom-call | flops 8589934592 | bytes 4194304 | tf_op jit(solution)/shard_map/near_half/pallas_call | solution.py:413
  85.2 0.0 collective-permute-done.7.state_ref
  85.2 0.0 copy-done.4
  85.2 0.0 copy-done.5
  85.2 5.3 %tail.1 = bf16[64,512]{1,0:T(8,128)(2,1)} custom-call(bf16[16,64,512]{2,1,0:T(8,128)(2,1)S(1)} %first_state.1.first_ref, bf16[512,512]{1,0:T(8,128)(2,1)S(1)} %get-tuple-element.8.absorbed_ref, f32[512,512]{1,0:T(8,128)S(1)} %get-tuple-element.9.mixed_ref, f32[512,128]{1,0:T(8,128)S(1)} %get-tuple-element.10.stat_ref, ...), custom_call_target="tpu_custom_call" | custom-call | tf_op jit(solution)/shard_map/tail/pallas_call | solution.py:499
Async XLA Ops:
  0.0 5.0 %collective-permute-start.2 = (bf16[512,512]{1,0:T(8,128)(2,1)}, bf16[512,512]{1,0:T(8,128)(2,1)S(1)}, u32[]{:S(2)}, u32[]{:S(2)}) collective-permute-start(bf16[512,512]{1,0:T(8,128)(2,1)} %patch_a_hbm.1), channel_id=1, source_target_pairs={{0,1},{1,0},{2,3},{3,2},{4,5},{5,4},{6,7},{7,6},{8,9},{9,8},{10,11... | collective-permute-start | bytes 1572872 | tf_op jit(solution)/shard_map/ppermute | solution.py:543
  3.2 1.8 %collective-permute-start = (s32[512]{0:T(512)}, s32[512]{0:T(512)S(1)}, u32[]{:S(2)}, u32[]{:S(2)}) collective-permute-start(s32[512]{0:T(512)} %level_a_hbm.1), channel_id=1, source_target_pairs={{0,1},{1,0},{2,3},{3,2},{4,5},{5,4},{6,7},{7,6},{8,9},{9,8},{10,11... | collective-permute-start | bytes 6152 | tf_op jit(solution)/shard_map/ppermute | solution.py:543
  3.2 1.8 %collective-permute-start.1 = (s32[512]{0:T(512)}, s32[512]{0:T(512)S(1)}, u32[]{:S(2)}, u32[]{:S(2)}) collective-permute-start(s32[512]{0:T(512)} %sheet_a_hbm.1), channel_id=1, source_target_pairs={{0,1},{1,0},{2,3},{3,2},{4,5},{5,4},{6,7},{7,6},{8,9},{9,8},{10,11... | collective-permute-start | bytes 6152 | tf_op jit(solution)/shard_map/ppermute | solution.py:543
  5.0 0.6 copy-start.8
  5.0 0.6 copy-start.9
  5.0 0.8 copy-start.7
  5.8 54.5 %copy-start.1 = (bf16[4,512,512]{2,1,0:T(8,128)(2,1)S(1)}, bf16[4,512,512]{2,1,0:T(8,128)(2,1)}, u32[]{:S(2)}) copy-start(bf16[4,512,512]{2,1,0:T(8,128)(2,1)} %proj_hbm.5) | copy-start | bytes 6291460
  21.1 39.1 %copy-start = (bf16[2048,512]{1,0:T(8,128)(2,1)S(1)}, bf16[2048,512]{1,0:T(8,128)(2,1)}, u32[]{:S(2)}) copy-start(bf16[2048,512]{1,0:T(8,128)(2,1)} %param.12) | copy-start | bytes 6291460
  21.2 39.1 %copy-start.6 = (f32[3,512]{1,0:T(4,128)S(1)}, f32[3,512]{1,0:T(4,128)}, u32[]{:S(2)}) copy-start(f32[3,512]{1,0:T(4,128)} %gain_ref.3) | copy-start | bytes 18436
  44.5 3.5 %collective-permute-start.3 = (bf16[72,512]{1,0:T(8,128)(2,1)S(1)}, bf16[72,512]{1,0:T(8,128)(2,1)S(1)}, u32[]{:S(2)}, u32[]{:S(2)}) collective-permute-start(bf16[72,512]{1,0:T(8,128)(2,1)S(1)} %merge.2.a_ref), channel_id=1, source_target_pairs={{0,32},{32,0},{64,96},{96,64},{128,160},{160,128},{192,224},{224,1... | collective-permute-start | bytes 221192 | tf_op jit(solution)/shard_map/ppermute | solution.py:551
  48.3 8.1 %collective-permute-start.6 = (bf16[72,512]{1,0:T(8,128)(2,1)S(1)}, bf16[72,512]{1,0:T(8,128)(2,1)S(1)}, u32[]{:S(2)}, u32[]{:S(2)}) collective-permute-start(bf16[72,512]{1,0:T(8,128)(2,1)S(1)} %merge.3.a_ref), channel_id=1, source_target_pairs={{0,160},{32,128},{64,224},{96,192},{128,32},{160,0},{192,96},{224,... | collective-permute-start | bytes 221192 | tf_op jit(solution)/shard_map/ppermute | solution.py:554
  54.7 5.6 %collective-permute-start.5 = (bf16[72,512]{1,0:T(8,128)(2,1)S(1)}, bf16[72,512]{1,0:T(8,128)(2,1)S(1)}, u32[]{:S(2)}, u32[]{:S(2)}) collective-permute-start(bf16[72,512]{1,0:T(8,128)(2,1)S(1)} %merge.3.a_ref), channel_id=1, source_target_pairs={{0,224},{32,64},{64,32},{96,128},{128,96},{160,192},{192,160},{224... | collective-permute-start | bytes 221192 | tf_op jit(solution)/shard_map/ppermute | solution.py:554
  54.7 5.6 %collective-permute-start.4 = (bf16[72,512]{1,0:T(8,128)(2,1)S(1)}, bf16[72,512]{1,0:T(8,128)(2,1)S(1)}, u32[]{:S(2)}, u32[]{:S(2)}) collective-permute-start(bf16[72,512]{1,0:T(8,128)(2,1)S(1)} %merge.3.a_ref), channel_id=1, source_target_pairs={{0,192},{32,96},{64,0},{96,160},{128,64},{160,224},{192,128},{224,... | collective-permute-start | bytes 221192 | tf_op jit(solution)/shard_map/ppermute | solution.py:554
  60.3 22.4 %copy-start.3 = (bf16[4,512,512]{2,1,0:T(8,128)(2,1)S(1)}, bf16[4,512,512]{2,1,0:T(8,128)(2,1)}, u32[]{:S(2)}) copy-start(bf16[4,512,512]{2,1,0:T(8,128)(2,1)} %proj_hbm.7) | copy-start | bytes 6291460
  61.4 21.3 %copy-start.2 = (bf16[2048,512]{1,0:T(8,128)(2,1)S(1)}, bf16[2048,512]{1,0:T(8,128)(2,1)}, u32[]{:S(2)}) copy-start(bf16[2048,512]{1,0:T(8,128)(2,1)} %param.13) | copy-start | bytes 6291460
  77.9 7.3 %copy-start.4 = (bf16[512,2048]{1,0:T(8,128)(2,1)S(1)}, bf16[512,2048]{1,0:T(8,128)(2,1)}, u32[]{:S(2)}) copy-start(bf16[512,2048]{1,0:T(8,128)(2,1)} %mlp_in_hbm.1) | copy-start | bytes 6291460
  77.9 7.3 %copy-start.5 = (bf16[2048,512]{1,0:T(8,128)(2,1)S(1)}, bf16[2048,512]{1,0:T(8,128)(2,1)}, u32[]{:S(2)}) copy-start(bf16[2048,512]{1,0:T(8,128)(2,1)} %mlp_out_hbm.1) | copy-start | bytes 6291460
  77.9 7.3 %collective-permute-start.7 = (bf16[16,64,512]{2,1,0:T(8,128)(2,1)S(1)}, bf16[16,64,512]{2,1,0:T(8,128)(2,1)S(1)}, u32[]{:S(2)}, u32[]{:S(2)}) collective-permute-start(bf16[16,64,512]{2,1,0:T(8,128)(2,1)S(1)} %all_to_all.11.state_ref), channel_id=1, source_target_pairs={{0,1},{1,0},{2,3},{3,2},{4,5},{5,4},{6,7},{7,6},{8,9},{9,8},{10,11... | collective-permute-start | bytes 3145736 | tf_op jit(solution)/shard_map/ppermute | solution.py:566
